TPU v7x, 32 devices: a whole 2x2x4 slice. The times are simulated.
32 devices in a mesh: groups: 2 (over x), seq: 8 (over z, y), head: 2 (over core).
Axes of the slice: x: 2, y: 2, z: 4, core: 2. Of those that a mesh axis runs over, the one named last changes fastest.
Arguments:
- queries: bfloat16 [16384, 1536], P(('groups', 'seq', 'head')), parts along dimension 0, may hold values from -5 to 5
- keys: bfloat16 [16384, 1536], P(('groups', 'seq', 'head')), parts along dimension 0, may hold values from -5 to 5
- values: bfloat16 [16384, 1536], P(('groups', 'seq', 'head')), parts along dimension 0, may hold values from -6 to 6
- tile_lists: int32 [256, 24], P('groups'), parts along dimension 0, may hold values from 0 to 127, as said below
Outputs:
- attended: bfloat16 [16384, 1536], P(('groups', 'seq', 'head')), parts along dimension 0
There are 2 independent parts, one for each index of `groups`. A program takes and returns all parts, laid end to end along the dimension named above; each array names one. Nothing has to cross between parts.
Inputs may be any that keep to these rules, and one draw needn't show every extreme that they name: `tile_lists`: each row names 24 distinct tiles. Cut the tiles into runs of 16 consecutive ones: the rows of one run together name at most 8 distinct tiles of any run, exactly 8 tiles of half of the runs and 4 of the others.
All inputs are finite; a program needn't handle non-finite values.
Results may differ from a plain program's by a relative error of at most 0.0042.
Values may be sent and summed in bfloat16 or wider, within the bound.
No kernel may reach another device: no remote copies, remote signals or barrier semaphores. Data moves between devices by JAX's collectives and lax.ppermute only.
A program may use at most 128 MiB of HBM per device.

v0:
```python
import functools
import math

import jax
import jax.numpy as jnp
from jax import lax
from jax.experimental import pallas as pl
from jax.experimental.pallas import tpu as pltpu
from jax.sharding import Mesh, PartitionSpec as P

HD = 128
TILE = 64


def score_tile(key_flat, score_scale, query_tile, row_index):
    gathered = key_flat[row_index]
    scores = (
        jnp.einsum("qhd,khtd->hqkt", query_tile, gathered, preferred_element_type=jnp.float32)
        * score_scale
    )
    row_top = jnp.max(scores, axis=(2, 3), keepdims=True)
    weights = jnp.exp(scores - row_top)
    row_total = jnp.sum(weights, axis=(2, 3))
    return (weights.astype(jnp.bfloat16), row_total)


def mix_tile(value_flat, rounded, row_total, row_index):
    gathered = value_flat[row_index]
    mixture = jnp.einsum("hqkt,khtd->qhd", rounded, gathered, preferred_element_type=jnp.float32)
    mixture = mixture / jnp.transpose(row_total)[:, :, None]
    return mixture.astype(jnp.bfloat16).reshape(mixture.shape[0], -1)


def select_slots(
    pick_table, arrays, seq_count, capacity, shard_tiles, tile_rows, local_heads, head_dim
):
    count = len(arrays)
    stacked = jnp.stack(arrays, 0).reshape(count, shard_tiles, tile_rows, local_heads, head_dim)
    stacked = stacked.transpose(1, 0, 3, 2, 4).reshape(shard_tiles, -1)
    outgoing = jnp.dot(pick_table, stacked, preferred_element_type=jnp.float32).astype(jnp.bfloat16)
    return outgoing.reshape(seq_count, capacity, count, local_heads, tile_rows, head_dim)


def slot_plan(queries, keys, values, tile_lists):
    seq_count = lax.axis_size("seq")
    head_count = lax.axis_size("head")
    head_dim = HD
    tile_rows = TILE
    total_tiles, top_count = tile_lists.shape
    local_heads = queries.shape[1] // head_dim // head_count
    local_rows = queries.shape[0] * head_count
    shard_tiles = local_rows // tile_rows
    capacity = 64 // seq_count
    seq_index = lax.axis_index("seq")
    score_scale = head_dim ** (-0.5)
    tile_ids = seq_index * shard_tiles + jnp.arange(shard_tiles, dtype=jnp.int32)
    by_run = tile_lists.reshape(seq_count, shard_tiles * top_count)
    need_out = jnp.any(by_run[:, :, None] == tile_ids[None, None, :], axis=1)
    slot_out = jnp.cumsum(need_out.astype(jnp.int32), axis=1) - 1
    slot_ids = jnp.arange(capacity, dtype=jnp.int32)
    pick_table = need_out[:, None, :] & (slot_out[:, None, :] == slot_ids[None, :, None])
    pick_table = pick_table.astype(jnp.bfloat16).reshape(seq_count * capacity, shard_tiles)
    own_lists = lax.dynamic_slice_in_dim(tile_lists, seq_index * shard_tiles, shard_tiles, 0)
    all_ids = jnp.arange(total_tiles, dtype=jnp.int32)
    matches = own_lists[:, :, None] == all_ids[None, None, :]
    listed = jnp.any(matches, axis=1).reshape(shard_tiles, seq_count, shard_tiles)
    need_in = jnp.any(listed, axis=0)
    slot_in = jnp.cumsum(need_in.astype(jnp.int32), axis=1) - 1
    queries_local, keys_local, values_local = (
        lax.all_to_all(queries, "head", split_axis=1, concat_axis=0, tiled=True),
        lax.all_to_all(keys, "head", split_axis=1, concat_axis=0, tiled=True),
        lax.all_to_all(values, "head", split_axis=1, concat_axis=0, tiled=True),
    )
    received = lax.all_to_all(
        select_slots(
            pick_table,
            (keys_local, values_local),
            seq_count,
            capacity,
            shard_tiles,
            tile_rows,
            local_heads,
            head_dim,
        ),
        "seq",
        split_axis=0,
        concat_axis=0,
        tiled=True,
    )
    key_slots = received[:, :, 0]
    value_slots = received[:, :, 1]
    flat_slots = jnp.broadcast_to(slot_in.reshape(1, 1, total_tiles), matches.shape)
    listed_slot = jnp.sum(jnp.where(matches, flat_slots, 0), axis=2)
    source_run = own_lists // shard_tiles
    slot_index = source_run * capacity + listed_slot
    query_tiles = queries_local.reshape(shard_tiles, tile_rows, local_heads, head_dim)
    slot_shape = (seq_count * capacity, local_heads, tile_rows, head_dim)
    key_flat = key_slots.reshape(slot_shape)
    value_flat = value_slots.reshape(slot_shape)

    def joined_tile(args):
        rounded, row_total = score_tile(key_flat, score_scale, args[0], args[1])
        return mix_tile(value_flat, rounded, row_total, args[1])

    attended = lax.map(joined_tile, (query_tiles, slot_index))
    attended = attended.reshape(local_rows, local_heads * head_dim)
    return lax.all_to_all(attended, "head", split_axis=0, concat_axis=1, tiled=True)


PLANES = 4
SIDE = 2
AXES = ("groups", "z", "y", "head")
RANKS = ("y", "head")
INWARD = [(0, 1), (3, 2)]
OUTWARD = [(1, 0), (2, 3)]
CROSS = [(1, 2), (2, 1)]
EXPONENT = HD**-0.5 * math.log2(math.e)
UNROLL = 4
COST = 9 * 10**9
LONG = 24 * 10**9
VMEM_LIMIT = 60 * 1024 * 1024


def shuffle_kernel(*refs, parts, source_count):
    sources, outs = refs[:source_count], refs[source_count : source_count + len(parts)]
    bufs, sems = refs[source_count + len(parts) : -1], refs[-1]
    loads, stores = {}, []
    for wanted in parts:
        for which, chunk in wanted:
            width = outs[0].shape[0] * HD
            columns = pl.ds(chunk * width, width)
            loads[which, chunk] = pltpu.make_async_copy(
                sources[which].at[:, columns], bufs[which].at[:, columns], sems.at[len(loads)]
            )
            loads[which, chunk].start()
    for out, wanted in zip(outs, parts):
        for at, (which, chunk) in enumerate(wanted):
            loads[which, chunk].wait()
            for lane in range(out.shape[0]):
                column = (chunk * out.shape[0] + lane) * HD
                store = pltpu.make_async_copy(
                    bufs[which].at[:, pl.ds(column, HD)],
                    out.at[lane, at],
                    sems.at[len(loads) + len(stores)],
                )
                store.start()
                stores.append(store)
    for store in stores:
        store.wait()


def shuffle(arrays, lanes, parts, name):
    rows = arrays[0].shape[0]
    kernel = functools.partial(shuffle_kernel, parts=parts, source_count=len(arrays))
    moved = sum(len(p) for p in parts)
    return pl.pallas_call(
        kernel,
        out_shape=[
            jax.ShapeDtypeStruct((lanes, len(p), rows, HD), arrays[0].dtype) for p in parts
        ],
        in_specs=[pl.BlockSpec(memory_space=pl.ANY)] * len(arrays),
        out_specs=[pl.BlockSpec(memory_space=pl.ANY)] * len(parts),
        scratch_shapes=[pltpu.VMEM(a.shape, a.dtype) for a in arrays]
        + [pltpu.SemaphoreType.DMA((moved * (lanes + 1),))],
        compiler_params=pltpu.CompilerParams(vmem_limit_bytes=VMEM_LIMIT),
        cost_estimate=pl.CostEstimate(
            flops=0, bytes_accessed=2 * moved * lanes * rows * HD * 2, transcendentals=0
        ),
        name=name,
    )(*arrays)


def gather_kernel(*refs):
    sources, out, buf, sems = refs[:-3], refs[-3], refs[-2], refs[-1]
    loads = []
    for source in sources:
        for at in range(source.shape[1]):
            for lane in range(source.shape[0]):
                column = pl.ds(len(loads) * HD, HD)
                load = pltpu.make_async_copy(
                    source.at[lane, at], buf.at[:, column], sems.at[len(loads)]
                )
                load.start()
                loads.append(load)
    for load in loads:
        load.wait()
    store = pltpu.make_async_copy(buf, out, sems.at[len(loads)])
    store.start()
    store.wait()


def gather_out(parts):
    rows = parts[0].shape[2]
    blocks = sum(p.shape[0] * p.shape[1] for p in parts)
    return pl.pallas_call(
        gather_kernel,
        out_shape=jax.ShapeDtypeStruct((rows, blocks * HD), parts[0].dtype),
        in_specs=[pl.BlockSpec(memory_space=pl.ANY)] * len(parts),
        out_specs=pl.BlockSpec(memory_space=pl.ANY),
        scratch_shapes=[
            pltpu.VMEM((rows, blocks * HD), parts[0].dtype),
            pltpu.SemaphoreType.DMA((blocks + 1,)),
        ],
        compiler_params=pltpu.CompilerParams(vmem_limit_bytes=VMEM_LIMIT),
        name="gather_out",
    )(*parts)


def attend_kernel(count, lists, query, *refs, chunk, ats):
    picks = refs[: 2 * PLANES]
    out, query_buf, key_buf, value_buf, score_buf, sems = refs[2 * PLANES :]
    lanes, _, shard_tiles = query.shape[:3]
    tiles = lanes * shard_tiles
    top_count = lists.shape[1]
    blank = jnp.zeros((TILE, HD), jnp.bfloat16)

    def beside(left, right):
        return jnp.concatenate([left, right], axis=1)

    @pl.when(count[0] > 0)
    def _():
        for lane in range(lanes):
            place = pl.ds(lane * shard_tiles, shard_tiles)
            pltpu.make_async_copy(query.at[lane, chunk], query_buf.at[place], sems.at[0]).start()
        for kind, buf in enumerate((key_buf, value_buf)):
            for slot in range(PLANES):
                source, at = picks[kind * PLANES + slot], ats[kind]
                for lane in range(lanes):
                    place = pl.ds((slot * lanes + lane) * shard_tiles, shard_tiles)
                    pltpu.make_async_copy(
                        source.at[lane, at], buf.at[place], sems.at[1 + kind]
                    ).start()
        pltpu.make_async_copy(query_buf, query_buf, sems.at[0]).wait()
        pltpu.make_async_copy(key_buf, key_buf, sems.at[1]).wait()

        def listed(buf, pair, t):
            return beside(buf[lists[2 * pair, t]], buf[lists[2 * pair + 1, t]])

        def score(pair, at):
            wide = jnp.concatenate(
                [beside(query_buf[2 * pair], blank), beside(blank, query_buf[2 * pair + 1])], axis=0
            )
            keys = jnp.concatenate([listed(key_buf, pair, t) for t in range(top_count)], axis=0)
            score_buf[at] = lax.dot_general(
                wide, keys, (((1,), (1,)), ((), ())), preferred_element_type=jnp.float32
            )

        def mix(pair, at):
            scores = score_buf[at]
            row_top = jnp.max(scores, axis=1, keepdims=True)
            weights = jnp.exp2((scores - row_top) * EXPONENT)
            row_total = jnp.sum(weights, axis=1, keepdims=True)
            values = jnp.concatenate([listed(value_buf, pair, t) for t in range(top_count)], axis=0)
            mixture = jnp.dot(
                weights.astype(jnp.bfloat16), values, preferred_element_type=jnp.float32
            )
            first = mixture[:TILE, :HD] / row_total[:TILE]
            second = mixture[TILE:, HD:] / row_total[TILE:]
            out[2 * pair] = first.astype(jnp.bfloat16)
            out[2 * pair + 1] = second.astype(jnp.bfloat16)

        score(0, 0)
        pltpu.make_async_copy(value_buf, value_buf, sems.at[2]).wait()

        unroll = math.gcd(tiles // 2, UNROLL)

        def step(at, carry):
            for sub in range(unroll):
                pair = at * unroll + sub
                score(jnp.minimum(pair + 1, tiles // 2 - 1), (sub + 1) % 2)
                mix(pair, sub % 2)
            return carry

        lax.fori_loop(0, tiles // 2 // unroll, step, 0)


def attend(count, lists, query, keys, values, ats, chunk, cost, name):
    tiles, top_count = lists.shape
    lanes = query.shape[0]
    shaped = (lanes, -1, tiles // lanes, TILE, HD)
    return pl.pallas_call(
        functools.partial(attend_kernel, chunk=chunk, ats=ats),
        out_shape=jax.ShapeDtypeStruct((tiles, TILE, HD), jnp.bfloat16),
        in_specs=[pl.BlockSpec(memory_space=pltpu.SMEM)] * 2
        + [pl.BlockSpec(memory_space=pl.ANY)] * (1 + 2 * PLANES),
        out_specs=pl.BlockSpec(memory_space=pltpu.VMEM),
        scratch_shapes=[
            pltpu.VMEM((tiles, TILE, HD), jnp.bfloat16),
            pltpu.VMEM((PLANES * tiles, TILE, HD), jnp.bfloat16),
            pltpu.VMEM((PLANES * tiles, TILE, HD), jnp.bfloat16),
            pltpu.VMEM((2, 2 * TILE, top_count * TILE), jnp.float32),
            pltpu.SemaphoreType.DMA((3,)),
        ],
        compiler_params=pltpu.CompilerParams(vmem_limit_bytes=VMEM_LIMIT),
        cost_estimate=pl.CostEstimate(flops=cost, bytes_accessed=1, transcendentals=0),
        name=name,
    )(count, lists, query.reshape(shaped), *[a.reshape(shaped) for a in (*keys, *values)])


def after(array, *others):
    return lax.optimization_barrier((array, *others))[0]


def relay_plan(queries, keys, values, tile_lists):
    z = lax.axis_index("z")
    lanes = SIDE * lax.axis_size("head")
    chunks = queries.shape[1] // (lanes * HD)
    plane_tiles = tile_lists.shape[0] // PLANES
    at_end = (z == 0) | (z == PLANES - 1)

    def swap(array):
        return lax.all_to_all(array, RANKS, split_axis=0, concat_axis=0, tiled=True)

    def send(array, pairs, name):
        with jax.named_scope(name):
            return lax.ppermute(array, "z", pairs)

    far = z >= PLANES // 2
    rows = jnp.stack(
        [
            lax.dynamic_slice_in_dim(tile_lists, z * plane_tiles, plane_tiles, 0),
            lax.dynamic_slice_in_dim(tile_lists, (z ^ 1) * plane_tiles, plane_tiles, 0),
        ]
    )
    plane = rows // plane_tiles
    plane = jnp.where(far, PLANES - 1 - plane, plane)
    near = jnp.where(far, PLANES - 1 - z, z)
    slot = jnp.where(plane < 2, plane ^ near, plane)
    lists = slot * plane_tiles + rows % plane_tiles
    count = jnp.where(at_end, 0, 1).astype(jnp.int32).reshape(1)

    (first,) = shuffle([keys, values], lanes, [[(0, 0), (1, 0)]], "shuffle_first")
    own_0 = swap(first)
    rest_1, rest_q0, rest_2, rest_q = shuffle(
        [queries, keys, values],
        lanes,
        [[(1, 1), (2, 1)], [(0, 0), (0, 1)], [(1, 2), (2, 2)], [(0, 2)]],
        "shuffle_rest",
    )
    in_0 = send(own_0, INWARD, "in_0")
    cross_0 = send(own_0, CROSS, "cross_0")
    own_1 = swap(after(rest_1, own_0))
    relay_0 = send(after(in_0, cross_0), CROSS, "relay_0")
    in_1 = send(after(own_1, in_0), INWARD, "in_1")
    cross_1 = send(after(own_1, cross_0), CROSS, "cross_1")
    asked_0 = swap(after(rest_q0, own_1, cross_0, in_0))
    in_q0 = send(after(asked_0, in_0), INWARD, "in_q0")
    own_2 = swap(after(rest_2, asked_0))
    relay_1 = send(after(in_1, relay_0), CROSS, "relay_1")
    in_2 = send(after(own_2, in_1), INWARD, "in_2")
    cross_2 = send(after(own_2, relay_0, cross_1), CROSS, "cross_2")
    asked = swap(after(rest_q, own_2))
    in_q = send(after(asked, in_q0), INWARD, "in_q")
    relay_2 = send(after(in_2, relay_1), CROSS, "relay_2")

    def one(at, chunk, query, pairs, place, cost=COST):
        name = f"attend_{chunk}{at}"
        return attend(count, lists[at], query, pairs, pairs, (0, 1), place, cost, name)

    def home(beside, chunk):
        return send(beside, OUTWARD, f"out_{chunk}")

    def finish(parts):
        mixed = []
        for own, home in parts:
            mixed.append(jnp.where(at_end, home, own).reshape(lanes, -1, HD))
        return mixed[0][:, None] if len(mixed) == 1 else jnp.stack(mixed, axis=1)

    pairs = [own_0, in_0, cross_0, relay_0]
    mine_0 = one(0, 0, asked_0, pairs, 0)
    theirs_0 = one(1, 0, after(in_q0, mine_0), pairs, 0)
    home_0 = home(theirs_0, 0)
    pairs = [own_1, in_1, cross_1, relay_1]
    mine_1 = one(0, 1, after(asked_0, theirs_0), pairs, 1)
    theirs_1 = one(1, 1, after(in_q0, mine_1), pairs, 1, LONG)
    home_1 = home(theirs_1, 1)
    mixed = finish([(mine_0, home_0), (mine_1, home_1)])
    early = swap(mixed)
    pairs = [own_2, in_2, cross_2, relay_2]
    theirs_2 = one(1, 2, after(in_q, theirs_1, mixed), pairs, 0, 1)
    mine_2 = one(0, 2, after(asked, theirs_2), pairs, 0, 1)
    late = swap(after(finish([(mine_2, home(theirs_2, 2))]), early))
    return gather_out([early, late])


def solution(mesh):
    seq_count, head_count = mesh.shape["seq"], mesh.shape["head"]
    if seq_count == PLANES * SIDE:
        planned = Mesh(mesh.devices.reshape(-1, PLANES, SIDE, head_count), AXES)
        plan, tokens = relay_plan, AXES
    else:
        planned, plan, tokens = mesh, slot_plan, ("groups", "seq", "head")
    placed = P(tokens, None)
    return jax.shard_map(
        plan,
        mesh=planned,
        in_specs=(placed, placed, placed, P("groups", None)),
        out_specs=placed,
        check_vma=False,
    )
```

profile of v0, /device:TPU:18, one launch (start us, length us, event | category | flops | bytes accessed | tf_op | source)
XLA Modules:
  0.0 208.1 jit_solution(4952887191163253770)
XLA Ops:
  0.0 2.1 %shuffle_first.1 = bf16[4,2,512,128]{3,2,1,0:T(8,128)(2,1)} custom-call(bf16[512,1536]{1,0:T(8,128)(2,1)} %refs_0_.3, bf16[512,1536]{1,0:T(8,128)(2,1)} %refs_1_.3), custom_call_target="tpu_custom_call" | custom-call | bytes 2097152 | tf_op jit(solution)/shard_map/shuffle_first/pallas_call | solution.py:156
  2.1 18.0 %all_to_all.35 = bf16[4,2,512,128]{3,2,1,0:T(8,128)(2,1)S(1)} all-to-all(bf16[4,2,512,128]{3,2,1,0:T(8,128)(2,1)} %shuffle_first.1), channel_id=1, replica_groups=mesh['groups'=2,'z'=4,'y'=2,'head'=2] {'y','head'}, dimensions={0} | all-to-all | bytes 2097152 | tf_op jit(solution)/shard_map/all_to_all | solution.py:312
  21.3 2.4 %collective-permute-start = (bf16[4,2,512,128]{3,2,1,0:T(8,128)(2,1)S(1)}, bf16[4,2,512,128]{3,2,1,0:T(8,128)(2,1)}, u32[]{:S(2)}, u32[]{:S(2)}) collective-permute-start(bf16[4,2,512,128]{3,2,1,0:T(8,128)(2,1)S(1)} %all_to_all.35), channel_id=1, source_target_pairs={{4,8},{8,4},{5,9},{9,5},{6,10},{10,6},{7,11},{11,7},{20,24},{24,20... | collective-permute-start | bytes 3145736 | tf_op jit(solution)/shard_map/cross_0/ppermute | solution.py:316
  23.7 3.3 %shuffle_rest.1 = (bf16[4,2,512,128]{3,2,1,0:T(8,128)(2,1)}, bf16[4,2,512,128]{3,2,1,0:T(8,128)(2,1)}, bf16[4,2,512,128]{3,2,1,0:T(8,128)(2,1)}, bf16[4,1,512,128]{3,2,1,0:T(8,128)(2,1)}) custom-call(bf16[512,1536]{1,0:T(8,128)(2,1)} %refs_0_.2, bf16[512,1536]{1,0:T(8,128)(2,1)} %refs_0_.3, bf16[512,1536]{1,0:T(8,128)(2,1)} %refs_1_.3), custom_call_target="tpu_custom_call" | custom-call | bytes 7340032 | tf_op jit(solution)/shard_map/shuffle_rest/pallas_call | solution.py:156
  27.0 3.5 %all-to-all-start.1 = ((bf16[4,2,512,128]{3,2,1,0:T(8,128)(2,1)}), bf16[4,2,512,128]{3,2,1,0:T(8,128)(2,1)S(1)}, u32[]{:S(2)}, u32[]{:S(2)}) async-start(bf16[4,2,512,128]{3,2,1,0:T(8,128)(2,1)} %get-tuple-element.30), calls=%async_computation.1 | async-start | bytes 2097152 | tf_op jit(solution)/shard_map/all_to_all | solution.py:312
  30.6 15.9 %collective-permute-done.1 = bf16[4,2,512,128]{3,2,1,0:T(8,128)(2,1)S(1)} collective-permute-done((bf16[4,2,512,128]{3,2,1,0:T(8,128)(2,1)S(1)}, bf16[4,2,512,128]{3,2,1,0:T(8,128)(2,1)S(1)}, u32[]{:S(2)}, u32[]{:S(2)}) %collective-permute-start.1) | collective-permute-done | bytes 1048608 | tf_op jit(solution)/shard_map/in_0/ppermute | solution.py:316
  47.9 2.3 %collective-permute-start.3 = (bf16[4,2,512,128]{3,2,1,0:T(8,128)(2,1)S(1)}, bf16[4,2,512,128]{3,2,1,0:T(8,128)(2,1)}, u32[]{:S(2)}, u32[]{:S(2)}) collective-permute-start(bf16[4,2,512,128]{3,2,1,0:T(8,128)(2,1)S(1)} %collective-permute-done.1), channel_id=1, source_target_pairs={{4,8},{8,4},{5,9},{9,5},{6,10},{10,6},{7,11},{11,7},{20,24},{24,20... | collective-permute-start | bytes 3145736 | tf_op jit(solution)/shard_map/relay_0/ppermute | solution.py:316
  51.6 4.3 %all-to-all-start.2 = ((bf16[4,2,512,128]{3,2,1,0:T(8,128)(2,1)}), bf16[4,2,512,128]{3,2,1,0:T(8,128)(2,1)}, u32[]{:S(2)}, u32[]{:S(2)}) async-start(bf16[4,2,512,128]{3,2,1,0:T(8,128)(2,1)} %get-tuple-element.31), calls=%async_computation.2 | async-start | bytes 2097152 | tf_op jit(solution)/shard_map/all_to_all | solution.py:312
  56.1 3.5 %collective-permute-start.6 = (bf16[4,2,512,128]{3,2,1,0:T(8,128)(2,1)S(1)}, bf16[4,2,512,128]{3,2,1,0:T(8,128)(2,1)}, u32[]{:S(2)}, u32[]{:S(2)}) collective-permute-start(bf16[4,2,512,128]{3,2,1,0:T(8,128)(2,1)S(1)} %all-to-all-done.1), channel_id=1, source_target_pairs={{4,8},{8,4},{5,9},{9,5},{6,10},{10,6},{7,11},{11,7},{20,24},{24,20... | collective-permute-start | bytes 3145736 | tf_op jit(solution)/shard_map/cross_1/ppermute | solution.py:316
  59.6 10.7 %all-to-all-done.2 = bf16[4,2,512,128]{3,2,1,0:T(8,128)(2,1)} async-done(((bf16[4,2,512,128]{3,2,1,0:T(8,128)(2,1)}), bf16[4,2,512,128]{3,2,1,0:T(8,128)(2,1)}, u32[]{:S(2)}, u32[]{:S(2)}) %all-to-all-start.2) | async-done | bytes 1048608 | tf_op jit(solution)/shard_map/all_to_all | solution.py:312
  72.3 3.5 %all-to-all-start.4 = ((bf16[4,2,512,128]{3,2,1,0:T(8,128)(2,1)}), bf16[4,2,512,128]{3,2,1,0:T(8,128)(2,1)S(1)}, u32[]{:S(2)}, u32[]{:S(2)}) async-start(bf16[4,2,512,128]{3,2,1,0:T(8,128)(2,1)} %get-tuple-element.42), calls=%async_computation.4 | async-start | bytes 2097152 | tf_op jit(solution)/shard_map/all_to_all | solution.py:312
  76.0 3.3 %collective-permute-start.7 = (bf16[4,2,512,128]{3,2,1,0:T(8,128)(2,1)}, bf16[4,2,512,128]{3,2,1,0:T(8,128)(2,1)}, u32[]{:S(2)}, u32[]{:S(2)}) collective-permute-start(bf16[4,2,512,128]{3,2,1,0:T(8,128)(2,1)} %collective-permute-done.5), channel_id=1, source_target_pairs={{4,8},{8,4},{5,9},{9,5},{6,10},{10,6},{7,11},{11,7},{20,24},{24,20... | collective-permute-start | bytes 3145736 | tf_op jit(solution)/shard_map/relay_1/ppermute | solution.py:316
  79.3 10.8 %attend_00.1 = bf16[32,64,128]{2,1,0:T(8,128)(2,1)} custom-call(s32[1]{0:T(128)} %bitcast.count, s32[32,24]{1,0:T(8,128)} %get-tuple-element.51.lists, bf16[4,2,8,64,128]{4,3,2,1,0:T(8,128)(2,1)} %bitcast.5.query, bf16[4,2,8,64,128]{4,3,2,1,0:T(8,128)(2,1)} %bitcast.47, bf16[4,2,8,64,128]{4,3,2,1,0:T(8,128)(2,1)} %bitcast.54, ...), custom_call_target="tpu_custom_call" | custom-call | flops 8999999488 | bytes 1 | tf_op jit(solution)/shard_map/attend_00/pallas_call | solution.py:281
  90.2 4.1 %all-to-all-start.5 = ((bf16[4,1,512,128]{3,2,1,0:T(8,128)(2,1)}), bf16[4,1,512,128]{3,2,1,0:T(8,128)(2,1)}, u32[]{:S(2)}, u32[]{:S(2)}) async-start(bf16[4,1,512,128]{3,2,1,0:T(8,128)(2,1)} %get-tuple-element.43), calls=%async_computation.5 | async-start | bytes 1048576 | tf_op jit(solution)/shard_map/all_to_all | solution.py:312
  95.7 2.8 %collective-permute-done.6 = bf16[4,2,512,128]{3,2,1,0:T(8,128)(2,1)} collective-permute-done((bf16[4,2,512,128]{3,2,1,0:T(8,128)(2,1)S(1)}, bf16[4,2,512,128]{3,2,1,0:T(8,128)(2,1)}, u32[]{:S(2)}, u32[]{:S(2)}) %collective-permute-start.6) | collective-permute-done | bytes 1048608 | tf_op jit(solution)/shard_map/cross_1/ppermute | solution.py:316
  98.4 2.3 %collective-permute-start.11 = (bf16[4,2,512,128]{3,2,1,0:T(8,128)(2,1)S(1)}, bf16[4,2,512,128]{3,2,1,0:T(8,128)(2,1)S(1)}, u32[]{:S(2)}, u32[]{:S(2)}) collective-permute-start(bf16[4,2,512,128]{3,2,1,0:T(8,128)(2,1)S(1)} %all-to-all-done.4), channel_id=1, source_target_pairs={{4,8},{8,4},{5,9},{9,5},{6,10},{10,6},{7,11},{11,7},{20,24},{24,20... | collective-permute-start | bytes 3145736 | tf_op jit(solution)/shard_map/cross_2/ppermute | solution.py:316
  100.8 10.8 %attend_01.1 = bf16[32,64,128]{2,1,0:T(8,128)(2,1)} custom-call(s32[1]{0:T(128)} %bitcast.count, s32[32,24]{1,0:T(8,128)} %get-tuple-element.52.lists, bf16[4,2,8,64,128]{4,3,2,1,0:T(8,128)(2,1)} %bitcast.10.query, bf16[4,2,8,64,128]{4,3,2,1,0:T(8,128)(2,1)} %bitcast.49, bf16[4,2,8,64,128]{4,3,2,1,0:T(8,128)(2,1)} %bitcast.56, ...), custom_call_target="tpu_custom_call" | custom-call | flops 8999999488 | bytes 1 | tf_op jit(solution)/shard_map/attend_01/pallas_call | solution.py:281
  111.6 2.1 %collective-permute-start.4 = (bf16[32,64,128]{2,1,0:T(8,128)(2,1)}, bf16[32,64,128]{2,1,0:T(8,128)(2,1)}, u32[]{:S(2)}, u32[]{:S(2)}) collective-permute-start(bf16[32,64,128]{2,1,0:T(8,128)(2,1)} %attend_01.1), channel_id=1, source_target_pairs={{4,0},{8,12},{5,1},{9,13},{6,2},{10,14},{7,3},{11,15},{20,16},{24,... | collective-permute-start | bytes 1572872 | tf_op jit(solution)/shard_map/out_0/ppermute | solution.py:316
  113.7 7.2 %collective-permute-done.7 = bf16[4,2,512,128]{3,2,1,0:T(8,128)(2,1)} collective-permute-done((bf16[4,2,512,128]{3,2,1,0:T(8,128)(2,1)}, bf16[4,2,512,128]{3,2,1,0:T(8,128)(2,1)}, u32[]{:S(2)}, u32[]{:S(2)}) %collective-permute-start.7) | collective-permute-done | bytes 1048608 | tf_op jit(solution)/shard_map/relay_1/ppermute | solution.py:316
  120.9 10.8 %attend_10.1 = bf16[32,64,128]{2,1,0:T(8,128)(2,1)} custom-call(s32[1]{0:T(128)} %bitcast.count, s32[32,24]{1,0:T(8,128)} %get-tuple-element.51.lists, bf16[4,2,8,64,128]{4,3,2,1,0:T(8,128)(2,1)} %bitcast.12.query, bf16[4,2,8,64,128]{4,3,2,1,0:T(8,128)(2,1)} %bitcast.43, bf16[4,2,8,64,128]{4,3,2,1,0:T(8,128)(2,1)} %bitcast.14.refs_1_.refs_5_, ...), custom_call_target="tpu_custom_call" | custom-call | flops 8999999488 | bytes 1 | tf_op jit(solution)/shard_map/attend_10/pallas_call | solution.py:281
  131.7 2.4 %collective-permute-start.12 = (bf16[4,2,512,128]{3,2,1,0:T(8,128)(2,1)S(1)}, bf16[4,2,512,128]{3,2,1,0:T(8,128)(2,1)}, u32[]{:S(2)}, u32[]{:S(2)}) collective-permute-start(bf16[4,2,512,128]{3,2,1,0:T(8,128)(2,1)S(1)} %collective-permute-done.10), channel_id=1, source_target_pairs={{4,8},{8,4},{5,9},{9,5},{6,10},{10,6},{7,11},{11,7},{20,24},{24,20... | collective-permute-start | bytes 3145736 | tf_op jit(solution)/shard_map/relay_2/ppermute | solution.py:316
  134.1 10.8 %attend_11.1 = bf16[32,64,128]{2,1,0:T(8,128)(2,1)} custom-call(s32[1]{0:T(128)} %bitcast.count, s32[32,24]{1,0:T(8,128)} %get-tuple-element.52.lists, bf16[4,2,8,64,128]{4,3,2,1,0:T(8,128)(2,1)} %bitcast.17.query, bf16[4,2,8,64,128]{4,3,2,1,0:T(8,128)(2,1)} %bitcast.45, bf16[4,2,8,64,128]{4,3,2,1,0:T(8,128)(2,1)} %bitcast.14.refs_1_.refs_5_, ...), custom_call_target="tpu_custom_call" | custom-call | flops 24000000000 | bytes 1 | tf_op jit(solution)/shard_map/attend_11/pallas_call | solution.py:281
  144.9 2.1 collective-permute-start.8
  149.5 3.7 %collective-permute-done.8 = bf16[32,64,128]{2,1,0:T(8,128)(2,1)} collective-permute-done((bf16[32,64,128]{2,1,0:T(8,128)(2,1)}, bf16[32,64,128]{2,1,0:T(8,128)(2,1)}, u32[]{:S(2)}, u32[]{:S(2)}) %collective-permute-start.8) | collective-permute-done | bytes 524320 | tf_op jit(solution)/shard_map/out_1/ppermute | solution.py:316
  154.3 4.1 %collective-permute-done.9 = bf16[4,1,512,128]{3,2,1,0:T(8,128)(2,1)S(1)} collective-permute-done((bf16[4,1,512,128]{3,2,1,0:T(8,128)(2,1)}, bf16[4,1,512,128]{3,2,1,0:T(8,128)(2,1)S(1)}, u32[]{:S(2)}, u32[]{:S(2)}) %collective-permute-start.9) | collective-permute-done | bytes 524320 | tf_op jit(solution)/shard_map/in_q/ppermute | solution.py:316
  158.4 4.9 %collective-permute-done.12 = bf16[4,2,512,128]{3,2,1,0:T(8,128)(2,1)} collective-permute-done((bf16[4,2,512,128]{3,2,1,0:T(8,128)(2,1)S(1)}, bf16[4,2,512,128]{3,2,1,0:T(8,128)(2,1)}, u32[]{:S(2)}, u32[]{:S(2)}) %collective-permute-start.12) | collective-permute-done | bytes 1048608 | tf_op jit(solution)/shard_map/relay_2/ppermute | solution.py:316
  163.4 10.8 %attend_21.1 = bf16[32,64,128]{2,1,0:T(8,128)(2,1)} custom-call(s32[1]{0:T(128)} %bitcast.count, s32[32,24]{1,0:T(8,128)} %get-tuple-element.52.lists, bf16[4,1,8,64,128]{4,3,2,1,0:T(8,128)(2,1)} %bitcast.51, bf16[4,2,8,64,128]{4,3,2,1,0:T(8,128)(2,1)} %bitcast.28, bf16[4,2,8,64,128]{4,3,2,1,0:T(8,128)(2,1)} %bitcast.32, ...), custom_call_target="tpu_custom_call" | custom-call | flops 1 | bytes 1 | tf_op jit(solution)/shard_map/attend_21/pallas_call | solution.py:281
  175.5 3.5 %all-to-all-start.3 = ((bf16[4,2,512,128]{3,2,1,0:T(8,128)(2,1)}), bf16[4,2,512,128]{3,2,1,0:T(8,128)(2,1)S(1)}, u32[]{:S(2)}, u32[]{:S(2)}) async-start(bf16[4,2,512,128]{3,2,1,0:T(8,128)(2,1)} %pad_maximum_fusion), calls=%async_computation.3 | async-start | bytes 2097152 | tf_op jit(solution)/shard_map/all_to_all | solution.py:312
  179.0 10.8 %attend_20.1 = bf16[32,64,128]{2,1,0:T(8,128)(2,1)} custom-call(s32[1]{0:T(128)} %bitcast.count, s32[32,24]{1,0:T(8,128)} %get-tuple-element.51.lists, bf16[4,1,8,64,128]{4,3,2,1,0:T(8,128)(2,1)} %bitcast.24.query, bf16[4,2,8,64,128]{4,3,2,1,0:T(8,128)(2,1)} %bitcast.30, bf16[4,2,8,64,128]{4,3,2,1,0:T(8,128)(2,1)} %bitcast.34, ...), custom_call_target="tpu_custom_call" | custom-call | flops 1 | bytes 1 | tf_op jit(solution)/shard_map/attend_20/pallas_call | solution.py:281
  191.0 2.5 %all-to-all-done.3.refs_0_ = bf16[4,2,512,128]{3,2,1,0:T(8,128)(2,1)S(1)} async-done(((bf16[4,2,512,128]{3,2,1,0:T(8,128)(2,1)}), bf16[4,2,512,128]{3,2,1,0:T(8,128)(2,1)S(1)}, u32[]{:S(2)}, u32[]{:S(2)}) %all-to-all-start.3) | async-done | bytes 1048608 | tf_op jit(solution)/shard_map/all_to_all | solution.py:312
  193.5 11.9 %all_to_all.36.refs_1_ = bf16[4,1,512,128]{3,2,1,0:T(8,128)(2,1)} all-to-all(bf16[4,1,512,128]{3,2,1,0:T(8,128)(2,1)S(1)} %bitcast.40), channel_id=1, replica_groups=mesh['groups'=2,'z'=4,'y'=2,'head'=2] {'y','head'}, dimensions={0} | all-to-all | bytes 1048576 | tf_op jit(solution)/shard_map/all_to_all | solution.py:312
  205.4 2.7 %gather_out.1 = bf16[512,1536]{1,0:T(8,128)(2,1)} custom-call(bf16[4,2,512,128]{3,2,1,0:T(8,128)(2,1)} %copy-done.3, bf16[4,1,512,128]{3,2,1,0:T(8,128)(2,1)} %all_to_all.36.refs_1_), custom_call_target="tpu_custom_call" | custom-call | tf_op jit(solution)/shard_map/gather_out/pallas_call | solution.py:195
  (46 shorter events, 13.9 us)
Async XLA Ops:
  20.0 7.0 %copy-start.5 = (bf16[4,2,512,128]{3,2,1,0:T(8,128)(2,1)}, bf16[4,2,512,128]{3,2,1,0:T(8,128)(2,1)S(1)}, u32[]{:S(2)}) copy-start(bf16[4,2,512,128]{3,2,1,0:T(8,128)(2,1)S(1)} %all_to_all.35) | copy-start | bytes 3145732
  20.1 26.4 %collective-permute-start.1 = (bf16[4,2,512,128]{3,2,1,0:T(8,128)(2,1)S(1)}, bf16[4,2,512,128]{3,2,1,0:T(8,128)(2,1)S(1)}, u32[]{:S(2)}, u32[]{:S(2)}) collective-permute-start(bf16[4,2,512,128]{3,2,1,0:T(8,128)(2,1)S(1)} %all_to_all.35), channel_id=1, source_target_pairs={{0,4},{12,8},{1,5},{13,9},{2,6},{14,10},{3,7},{15,11},{16,20},{28,... | collective-permute-start | bytes 3145736 | tf_op jit(solution)/shard_map/in_0/ppermute | solution.py:316
  21.3 26.5 %collective-permute-start = (bf16[4,2,512,128]{3,2,1,0:T(8,128)(2,1)S(1)}, bf16[4,2,512,128]{3,2,1,0:T(8,128)(2,1)}, u32[]{:S(2)}, u32[]{:S(2)}) collective-permute-start(bf16[4,2,512,128]{3,2,1,0:T(8,128)(2,1)S(1)} %all_to_all.35), channel_id=1, source_target_pairs={{4,8},{8,4},{5,9},{9,5},{6,10},{10,6},{7,11},{11,7},{20,24},{24,20... | collective-permute-start | bytes 3145736 | tf_op jit(solution)/shard_map/cross_0/ppermute | solution.py:316
  27.0 23.2 %all-to-all-start.1 = ((bf16[4,2,512,128]{3,2,1,0:T(8,128)(2,1)}), bf16[4,2,512,128]{3,2,1,0:T(8,128)(2,1)S(1)}, u32[]{:S(2)}, u32[]{:S(2)}) async-start(bf16[4,2,512,128]{3,2,1,0:T(8,128)(2,1)} %get-tuple-element.30), calls=%async_computation.1 | async-start | bytes 2097152 | tf_op jit(solution)/shard_map/all_to_all | solution.py:312
  30.6 25.3 %copy-start.8 = (s32[128,24]{0,1:T(8,128)S(1)}, s32[128,24]{0,1:T(8,128)}, u32[]{:S(2)}) copy-start(s32[128,24]{0,1:T(8,128)} %param.7) | copy-start | bytes 36868
  46.5 25.8 %copy-start.9 = (bf16[4,2,512,128]{3,2,1,0:T(8,128)(2,1)}, bf16[4,2,512,128]{3,2,1,0:T(8,128)(2,1)S(1)}, u32[]{:S(2)}) copy-start(bf16[4,2,512,128]{3,2,1,0:T(8,128)(2,1)S(1)} %collective-permute-done.1) | copy-start | bytes 3145732
  47.9 28.1 %collective-permute-start.3 = (bf16[4,2,512,128]{3,2,1,0:T(8,128)(2,1)S(1)}, bf16[4,2,512,128]{3,2,1,0:T(8,128)(2,1)}, u32[]{:S(2)}, u32[]{:S(2)}) collective-permute-start(bf16[4,2,512,128]{3,2,1,0:T(8,128)(2,1)S(1)} %collective-permute-done.1), channel_id=1, source_target_pairs={{4,8},{8,4},{5,9},{9,5},{6,10},{10,6},{7,11},{11,7},{20,24},{24,20... | collective-permute-start | bytes 3145736 | tf_op jit(solution)/shard_map/relay_0/ppermute | solution.py:316
  50.2 22.0 %copy-start.4 = (bf16[4,2,512,128]{3,2,1,0:T(8,128)(2,1)}, bf16[4,2,512,128]{3,2,1,0:T(8,128)(2,1)S(1)}, u32[]{:S(2)}) copy-start(bf16[4,2,512,128]{3,2,1,0:T(8,128)(2,1)S(1)} %all-to-all-done.1) | copy-start | bytes 3145732
  50.3 25.7 %collective-permute-start.5 = (bf16[4,2,512,128]{3,2,1,0:T(8,128)(2,1)S(1)}, bf16[4,2,512,128]{3,2,1,0:T(8,128)(2,1)}, u32[]{:S(2)}, u32[]{:S(2)}) collective-permute-start(bf16[4,2,512,128]{3,2,1,0:T(8,128)(2,1)S(1)} %all-to-all-done.1), channel_id=1, source_target_pairs={{0,4},{12,8},{1,5},{13,9},{2,6},{14,10},{3,7},{15,11},{16,20},{28,... | collective-permute-start | bytes 3145736 | tf_op jit(solution)/shard_map/in_1/ppermute | solution.py:316
  51.6 18.8 %all-to-all-start.2 = ((bf16[4,2,512,128]{3,2,1,0:T(8,128)(2,1)}), bf16[4,2,512,128]{3,2,1,0:T(8,128)(2,1)}, u32[]{:S(2)}, u32[]{:S(2)}) async-start(bf16[4,2,512,128]{3,2,1,0:T(8,128)(2,1)} %get-tuple-element.31), calls=%async_computation.2 | async-start | bytes 2097152 | tf_op jit(solution)/shard_map/all_to_all | solution.py:312
  56.1 42.3 %collective-permute-start.6 = (bf16[4,2,512,128]{3,2,1,0:T(8,128)(2,1)S(1)}, bf16[4,2,512,128]{3,2,1,0:T(8,128)(2,1)}, u32[]{:S(2)}, u32[]{:S(2)}) collective-permute-start(bf16[4,2,512,128]{3,2,1,0:T(8,128)(2,1)S(1)} %all-to-all-done.1), channel_id=1, source_target_pairs={{4,8},{8,4},{5,9},{9,5},{6,10},{10,6},{7,11},{11,7},{20,24},{24,20... | collective-permute-start | bytes 3145736 | tf_op jit(solution)/shard_map/cross_1/ppermute | solution.py:316
  70.3 30.4 %collective-permute-start.2 = (bf16[4,2,512,128]{3,2,1,0:T(8,128)(2,1)}, bf16[4,2,512,128]{3,2,1,0:T(8,128)(2,1)}, u32[]{:S(2)}, u32[]{:S(2)}) collective-permute-start(bf16[4,2,512,128]{3,2,1,0:T(8,128)(2,1)} %all-to-all-done.2), channel_id=1, source_target_pairs={{0,4},{12,8},{1,5},{13,9},{2,6},{14,10},{3,7},{15,11},{16,20},{28,... | collective-permute-start | bytes 3145736 | tf_op jit(solution)/shard_map/in_q0/ppermute | solution.py:316
  72.3 18.0 %all-to-all-start.4 = ((bf16[4,2,512,128]{3,2,1,0:T(8,128)(2,1)}), bf16[4,2,512,128]{3,2,1,0:T(8,128)(2,1)S(1)}, u32[]{:S(2)}, u32[]{:S(2)}) async-start(bf16[4,2,512,128]{3,2,1,0:T(8,128)(2,1)} %get-tuple-element.42), calls=%async_computation.4 | async-start | bytes 2097152 | tf_op jit(solution)/shard_map/all_to_all | solution.py:312
  76.0 44.9 %collective-permute-start.7 = (bf16[4,2,512,128]{3,2,1,0:T(8,128)(2,1)}, bf16[4,2,512,128]{3,2,1,0:T(8,128)(2,1)}, u32[]{:S(2)}, u32[]{:S(2)}) collective-permute-start(bf16[4,2,512,128]{3,2,1,0:T(8,128)(2,1)} %collective-permute-done.5), channel_id=1, source_target_pairs={{4,8},{8,4},{5,9},{9,5},{6,10},{10,6},{7,11},{11,7},{20,24},{24,20... | collective-permute-start | bytes 3145736 | tf_op jit(solution)/shard_map/relay_1/ppermute | solution.py:316
  90.2 21.4 %copy-start = (bf16[4,2,512,128]{3,2,1,0:T(8,128)(2,1)}, bf16[4,2,512,128]{3,2,1,0:T(8,128)(2,1)S(1)}, u32[]{:S(2)}) copy-start(bf16[4,2,512,128]{3,2,1,0:T(8,128)(2,1)S(1)} %all-to-all-done.4) | copy-start | bytes 3145732
  90.2 56.8 %all-to-all-start.5 = ((bf16[4,1,512,128]{3,2,1,0:T(8,128)(2,1)}), bf16[4,1,512,128]{3,2,1,0:T(8,128)(2,1)}, u32[]{:S(2)}, u32[]{:S(2)}) async-start(bf16[4,1,512,128]{3,2,1,0:T(8,128)(2,1)} %get-tuple-element.43), calls=%async_computation.5 | async-start | bytes 1048576 | tf_op jit(solution)/shard_map/all_to_all | solution.py:312
  94.4 37.4 %collective-permute-start.10 = (bf16[4,2,512,128]{3,2,1,0:T(8,128)(2,1)S(1)}, bf16[4,2,512,128]{3,2,1,0:T(8,128)(2,1)S(1)}, u32[]{:S(2)}, u32[]{:S(2)}) collective-permute-start(bf16[4,2,512,128]{3,2,1,0:T(8,128)(2,1)S(1)} %all-to-all-done.4), channel_id=1, source_target_pairs={{0,4},{12,8},{1,5},{13,9},{2,6},{14,10},{3,7},{15,11},{16,20},{28,... | collective-permute-start | bytes 3145736 | tf_op jit(solution)/shard_map/in_2/ppermute | solution.py:316
  98.4 60.0 %collective-permute-start.11 = (bf16[4,2,512,128]{3,2,1,0:T(8,128)(2,1)S(1)}, bf16[4,2,512,128]{3,2,1,0:T(8,128)(2,1)S(1)}, u32[]{:S(2)}, u32[]{:S(2)}) collective-permute-start(bf16[4,2,512,128]{3,2,1,0:T(8,128)(2,1)S(1)} %all-to-all-done.4), channel_id=1, source_target_pairs={{4,8},{8,4},{5,9},{9,5},{6,10},{10,6},{7,11},{11,7},{20,24},{24,20... | collective-permute-start | bytes 3145736 | tf_op jit(solution)/shard_map/cross_2/ppermute | solution.py:316
  111.6 36.8 %collective-permute-start.4 = (bf16[32,64,128]{2,1,0:T(8,128)(2,1)}, bf16[32,64,128]{2,1,0:T(8,128)(2,1)}, u32[]{:S(2)}, u32[]{:S(2)}) collective-permute-start(bf16[32,64,128]{2,1,0:T(8,128)(2,1)} %attend_01.1), channel_id=1, source_target_pairs={{4,0},{8,12},{5,1},{9,13},{6,2},{10,14},{7,3},{11,15},{20,16},{24,... | collective-permute-start | bytes 1572872 | tf_op jit(solution)/shard_map/out_0/ppermute | solution.py:316
  131.7 13.2 %copy-start.1 = (bf16[4,2,512,128]{3,2,1,0:T(8,128)(2,1)}, bf16[4,2,512,128]{3,2,1,0:T(8,128)(2,1)S(1)}, u32[]{:S(2)}) copy-start(bf16[4,2,512,128]{3,2,1,0:T(8,128)(2,1)S(1)} %collective-permute-done.10) | copy-start | bytes 3145732
  131.7 31.6 %collective-permute-start.12 = (bf16[4,2,512,128]{3,2,1,0:T(8,128)(2,1)S(1)}, bf16[4,2,512,128]{3,2,1,0:T(8,128)(2,1)}, u32[]{:S(2)}, u32[]{:S(2)}) collective-permute-start(bf16[4,2,512,128]{3,2,1,0:T(8,128)(2,1)S(1)} %collective-permute-done.10), channel_id=1, source_target_pairs={{4,8},{8,4},{5,9},{9,5},{6,10},{10,6},{7,11},{11,7},{20,24},{24,20... | collective-permute-start | bytes 3145736 | tf_op jit(solution)/shard_map/relay_2/ppermute | solution.py:316
  144.9 8.3 %collective-permute-start.8 = (bf16[32,64,128]{2,1,0:T(8,128)(2,1)}, bf16[32,64,128]{2,1,0:T(8,128)(2,1)}, u32[]{:S(2)}, u32[]{:S(2)}) collective-permute-start(bf16[32,64,128]{2,1,0:T(8,128)(2,1)} %attend_11.1), channel_id=1, source_target_pairs={{4,0},{8,12},{5,1},{9,13},{6,2},{10,14},{7,3},{11,15},{20,16},{24,... | collective-permute-start | bytes 1572872 | tf_op jit(solution)/shard_map/out_1/ppermute | solution.py:316
  147.0 6.2 %copy-start.7 = (bf16[32,64,128]{2,1,0:T(8,128)(2,1)S(1)}, bf16[32,64,128]{2,1,0:T(8,128)(2,1)}, u32[]{:S(2)}) copy-start(bf16[32,64,128]{2,1,0:T(8,128)(2,1)} %attend_10.1) | copy-start | bytes 1572868
  147.0 11.4 %collective-permute-start.9 = (bf16[4,1,512,128]{3,2,1,0:T(8,128)(2,1)}, bf16[4,1,512,128]{3,2,1,0:T(8,128)(2,1)S(1)}, u32[]{:S(2)}, u32[]{:S(2)}) collective-permute-start(bf16[4,1,512,128]{3,2,1,0:T(8,128)(2,1)} %all-to-all-done.5), channel_id=1, source_target_pairs={{0,4},{12,8},{1,5},{13,9},{2,6},{14,10},{3,7},{15,11},{16,20},{28,... | collective-permute-start | bytes 1572872 | tf_op jit(solution)/shard_map/in_q/ppermute | solution.py:316
  158.4 5.0 %copy-start.6 = (bf16[4,1,512,128]{3,2,1,0:T(8,128)(2,1)}, bf16[4,1,512,128]{3,2,1,0:T(8,128)(2,1)S(1)}, u32[]{:S(2)}) copy-start(bf16[4,1,512,128]{3,2,1,0:T(8,128)(2,1)S(1)} %collective-permute-done.9) | copy-start | bytes 1572868
  158.4 4.9 %copy-start.2 = (bf16[4,2,512,128]{3,2,1,0:T(8,128)(2,1)}, bf16[4,2,512,128]{3,2,1,0:T(8,128)(2,1)S(1)}, u32[]{:S(2)}) copy-start(bf16[4,2,512,128]{3,2,1,0:T(8,128)(2,1)S(1)} %collective-permute-done.11) | copy-start | bytes 3145732
  174.2 15.7 %collective-permute-start.13 = (bf16[32,64,128]{2,1,0:T(8,128)(2,1)}, bf16[32,64,128]{2,1,0:T(8,128)(2,1)S(1)}, u32[]{:S(2)}, u32[]{:S(2)}) collective-permute-start(bf16[32,64,128]{2,1,0:T(8,128)(2,1)} %attend_21.1), channel_id=1, source_target_pairs={{4,0},{8,12},{5,1},{9,13},{6,2},{10,14},{7,3},{11,15},{20,16},{24,... | collective-permute-start | bytes 1572872 | tf_op jit(solution)/shard_map/out_2/ppermute | solution.py:316
  175.5 18.0 %all-to-all-start.3 = ((bf16[4,2,512,128]{3,2,1,0:T(8,128)(2,1)}), bf16[4,2,512,128]{3,2,1,0:T(8,128)(2,1)S(1)}, u32[]{:S(2)}, u32[]{:S(2)}) async-start(bf16[4,2,512,128]{3,2,1,0:T(8,128)(2,1)} %pad_maximum_fusion), calls=%async_computation.3 | async-start | bytes 2097152 | tf_op jit(solution)/shard_map/all_to_all | solution.py:312
  193.5 11.9 %copy-start.3 = (bf16[4,2,512,128]{3,2,1,0:T(8,128)(2,1)}, bf16[4,2,512,128]{3,2,1,0:T(8,128)(2,1)S(1)}, u32[]{:S(2)}) copy-start(bf16[4,2,512,128]{3,2,1,0:T(8,128)(2,1)S(1)} %all-to-all-done.3.refs_0_) | copy-start | bytes 3145732
where the time goes:
time: 210 us; the launch traced here: 208 us
  Pallas kernels  72.8 us (35%)
  waiting for transfers between devices  53.5 us (25%)
  starting transfers between devices  47.2 us (22%)
  blocking collectives  29.9 us (14%)
  other arithmetic  3.39 us (2%)
    pallas_call x6, Pallas kernels, attend(): pl.pallas_call(functools.partial(attend_kernel, chunk=chunk, ats=ats), ou...  64.8 us
    ppermute x14, waiting for transfers between devices, send(): return lax.ppermute(array, 'z', pairs)  40.1 us
    all_to_all x2, blocking collectives, swap(): return lax.all_to_all(array, RANKS, split_axis=0, concat_axis=0, tiled=True)  29.9 us
    ppermute x14, starting transfers between devices, send(): return lax.ppermute(array, 'z', pairs)  28.3 us
    all_to_all x5, starting transfers between devices, swap(): return lax.all_to_all(array, RANKS, split_axis=0, concat_axis=0, tiled=True)  19 us
    all_to_all x5, waiting for transfers between devices, swap(): return lax.all_to_all(array, RANKS, split_axis=0, concat_axis=0, tiled=True)  13.4 us
    pallas_call x2, Pallas kernels, shuffle(): pl.pallas_call(kernel, out_shape=[jax.ShapeDtypeStruct((lanes, len(p), ro...  5.38 us
  transfers between devices with their start and end apart: 19, of which 11 were waited for; matrix products, arithmetic and copies ran while one was open for 2% of the time, Pallas kernels for 28%

commit v1 on v0

--- a/solution.py
+++ b/solution.py
@@ -170,40 +170,47 @@
     )(*arrays)
 
 
-def gather_kernel(*refs):
-    sources, out, buf, sems = refs[:-3], refs[-3], refs[-2], refs[-1]
-    loads = []
+def gather_kernel(*refs, first, held):
+    sources, out, buf, sems = refs[: len(refs) - 3 - held], refs[-3], refs[-2], refs[-1]
+    moves = []
     for source in sources:
         for at in range(source.shape[1]):
             for lane in range(source.shape[0]):
-                column = pl.ds(len(loads) * HD, HD)
+                here = pl.ds(len(moves) * HD, HD)
+                there = pl.ds((first + len(moves)) * HD, HD)
                 load = pltpu.make_async_copy(
-                    source.at[lane, at], buf.at[:, column], sems.at[len(loads)]
+                    source.at[lane, at], buf.at[:, here], sems.at[0, len(moves)]
                 )
                 load.start()
-                loads.append(load)
-    for load in loads:
+                store = pltpu.make_async_copy(
+                    buf.at[:, here], out.at[:, there], sems.at[1, len(moves)]
+                )
+                moves.append((load, store))
+    for load, store in moves:
         load.wait()
-    store = pltpu.make_async_copy(buf, out, sems.at[len(loads)])
-    store.start()
-    store.wait()
-
-
-def gather_out(parts):
+        store.start()
+    for load, store in moves:
+        store.wait()
+
+
+def gather_out(parts, first, total, held, name):
     rows = parts[0].shape[2]
     blocks = sum(p.shape[0] * p.shape[1] for p in parts)
+    given = [] if held is None else [held]
     return pl.pallas_call(
-        gather_kernel,
-        out_shape=jax.ShapeDtypeStruct((rows, blocks * HD), parts[0].dtype),
-        in_specs=[pl.BlockSpec(memory_space=pl.ANY)] * len(parts),
+        functools.partial(gather_kernel, first=first, held=len(given)),
+        out_shape=jax.ShapeDtypeStruct((rows, total * HD), parts[0].dtype),
+        in_specs=[pl.BlockSpec(memory_space=pl.ANY)] * (len(parts) + len(given)),
         out_specs=pl.BlockSpec(memory_space=pl.ANY),
         scratch_shapes=[
             pltpu.VMEM((rows, blocks * HD), parts[0].dtype),
-            pltpu.SemaphoreType.DMA((blocks + 1,)),
+            pltpu.SemaphoreType.DMA((2, blocks)),
         ],
+        input_output_aliases={len(parts): 0} if given else {},
         compiler_params=pltpu.CompilerParams(vmem_limit_bytes=VMEM_LIMIT),
-        name="gather_out",
-    )(*parts)
+        cost_estimate=pl.CostEstimate(flops=1, bytes_accessed=1, transcendentals=0),
+        name=name,
+    )(*parts, *given)
 
 
 def attend_kernel(count, lists, query, *refs, chunk, ats):
@@ -219,17 +226,15 @@
 
     @pl.when(count[0] > 0)
     def _():
-        for lane in range(lanes):
-            place = pl.ds(lane * shard_tiles, shard_tiles)
-            pltpu.make_async_copy(query.at[lane, chunk], query_buf.at[place], sems.at[0]).start()
+        shaped = (lanes, shard_tiles, TILE, HD)
+        pltpu.make_async_copy(query.at[:, chunk], query_buf.reshape(shaped), sems.at[0]).start()
         for kind, buf in enumerate((key_buf, value_buf)):
             for slot in range(PLANES):
-                source, at = picks[kind * PLANES + slot], ats[kind]
-                for lane in range(lanes):
-                    place = pl.ds((slot * lanes + lane) * shard_tiles, shard_tiles)
-                    pltpu.make_async_copy(
-                        source.at[lane, at], buf.at[place], sems.at[1 + kind]
-                    ).start()
+                pltpu.make_async_copy(
+                    picks[kind * PLANES + slot].at[:, ats[kind]],
+                    buf.reshape((PLANES, *shaped)).at[slot],
+                    sems.at[1 + kind],
+                ).start()
         pltpu.make_async_copy(query_buf, query_buf, sems.at[0]).wait()
         pltpu.make_async_copy(key_buf, key_buf, sems.at[1]).wait()
 
@@ -329,17 +334,20 @@
     lists = slot * plane_tiles + rows % plane_tiles
     count = jnp.where(at_end, 0, 1).astype(jnp.int32).reshape(1)
 
-    (first,) = shuffle([keys, values], lanes, [[(0, 0), (1, 0)]], "shuffle_first")
+    first, rest_2 = shuffle(
+        [keys, values], lanes, [[(0, 0), (1, 0)], [(0, 2), (1, 2)]], "shuffle_first"
+    )
+    raw_2 = send(rest_2, CROSS, "cross_raw_2")
     own_0 = swap(first)
-    rest_1, rest_q0, rest_2, rest_q = shuffle(
+    rest_1, rest_q0, rest_q = shuffle(
         [queries, keys, values],
         lanes,
-        [[(1, 1), (2, 1)], [(0, 0), (0, 1)], [(1, 2), (2, 2)], [(0, 2)]],
+        [[(1, 1), (2, 1)], [(0, 0)], [(0, 1), (0, 2)]],
         "shuffle_rest",
     )
     in_0 = send(own_0, INWARD, "in_0")
     cross_0 = send(own_0, CROSS, "cross_0")
-    own_1 = swap(after(rest_1, own_0))
+    own_1 = swap(after(rest_1, own_0, raw_2))
     relay_0 = send(after(in_0, cross_0), CROSS, "relay_0")
     in_1 = send(after(own_1, in_0), INWARD, "in_1")
     cross_1 = send(after(own_1, cross_0), CROSS, "cross_1")
@@ -348,10 +356,10 @@
     own_2 = swap(after(rest_2, asked_0))
     relay_1 = send(after(in_1, relay_0), CROSS, "relay_1")
     in_2 = send(after(own_2, in_1), INWARD, "in_2")
-    cross_2 = send(after(own_2, relay_0, cross_1), CROSS, "cross_2")
     asked = swap(after(rest_q, own_2))
     in_q = send(after(asked, in_q0), INWARD, "in_q")
-    relay_2 = send(after(in_2, relay_1), CROSS, "relay_2")
+    cross_2 = swap(after(raw_2, asked))
+    relay_2 = send(after(in_2, cross_1), CROSS, "relay_2")
 
     def one(at, chunk, query, pairs, place, cost=COST):
         name = f"attend_{chunk}{at}"
@@ -371,16 +379,16 @@
     theirs_0 = one(1, 0, after(in_q0, mine_0), pairs, 0)
     home_0 = home(theirs_0, 0)
     pairs = [own_1, in_1, cross_1, relay_1]
-    mine_1 = one(0, 1, after(asked_0, theirs_0), pairs, 1)
-    theirs_1 = one(1, 1, after(in_q0, mine_1), pairs, 1, LONG)
+    mine_1 = one(0, 1, after(asked, theirs_0, cross_2), pairs, 0)
+    theirs_1 = one(1, 1, after(in_q, mine_1), pairs, 0, LONG)
     home_1 = home(theirs_1, 1)
-    mixed = finish([(mine_0, home_0), (mine_1, home_1)])
+    pairs = [own_2, in_2, cross_2, relay_2]
+    theirs_2 = one(1, 2, after(in_q, theirs_1), pairs, 1, 1)
+    mixed = finish([(mine_0, home_0), (mine_1, after(home_1, theirs_2))])
     early = swap(mixed)
-    pairs = [own_2, in_2, cross_2, relay_2]
-    theirs_2 = one(1, 2, after(in_q, theirs_1, mixed), pairs, 0, 1)
-    mine_2 = one(0, 2, after(asked, theirs_2), pairs, 0, 1)
+    mine_2 = one(0, 2, after(asked, theirs_2), pairs, 1, 1)
     late = swap(after(finish([(mine_2, home(theirs_2, 2))]), early))
-    return gather_out([early, late])
+    return gather_out([early, late], 0, chunks * lanes, None, "gather_out")
 
 
 def solution(mesh):

time: 210 us -> 206 us (0.981)
  waiting for transfers between devices: 53.5 us -> 30.3 us
  blocking collectives: 29.9 us -> 48.6 us
    ppermute x14, waiting for transfers between devices: 40.1 us -> 20.1 us  [send(): return lax.ppermute(array, 'z', pairs)]
    all_to_all x2 -> x3, blocking collectives: 29.9 us -> 48.6 us  [swap(): return lax.all_to_all(array, RANKS, split_axis=0, concat_axis=0, tiled=True)]
    all_to_all x5, waiting for transfers between devices: 13.4 us -> 10.1 us  [swap(): return lax.all_to_all(array, RANKS, split_axis=0, concat_axis=0, tiled=True)]
  transfers between devices with their start and end apart: 19 -> 19, of which waited for: 11 -> 9; matrix products, arithmetic and copies ran while one was open for 2% -> 2% of each run, Pallas kernels for 28% -> 33%
where the time goes in v1:
time: 206 us; the launch traced here: 203 us
  Pallas kernels  72.1 us (35%)
  blocking collectives  48.6 us (24%)
  starting transfers between devices  46.1 us (22%)
  waiting for transfers between devices  30.3 us (15%)
  local copies, waits for them, and re-layouts  2.8 us (1%)
  other arithmetic  2.37 us (1%)
    pallas_call x6, Pallas kernels, attend(): pl.pallas_call(functools.partial(attend_kernel, chunk=chunk, ats=ats), ou...  64.6 us
    all_to_all x3, blocking collectives, swap(): return lax.all_to_all(array, RANKS, split_axis=0, concat_axis=0, tiled=True)  48.6 us
    ppermute x14, starting transfers between devices, send(): return lax.ppermute(array, 'z', pairs)  27.7 us
    ppermute x14, waiting for transfers between devices, send(): return lax.ppermute(array, 'z', pairs)  20.1 us
    all_to_all x5, starting transfers between devices, swap(): return lax.all_to_all(array, RANKS, split_axis=0, concat_axis=0, tiled=True)  18.3 us
    all_to_all x5, waiting for transfers between devices, swap(): return lax.all_to_all(array, RANKS, split_axis=0, concat_axis=0, tiled=True)  10.1 us
    pallas_call x2, Pallas kernels, shuffle(): pl.pallas_call(kernel, out_shape=[jax.ShapeDtypeStruct((lanes, len(p), ro...  5.23 us
  transfers between devices with their start and end apart: 19, of which 9 were waited for; matrix products, arithmetic and copies ran while one was open for 2% of the time, Pallas kernels for 33%

profile of v1, /device:TPU:18, one launch (start us, length us, event | category | flops | bytes accessed | tf_op | source)
XLA Modules:
  0.0 202.7 jit_solution(8430884165123600853)
XLA Ops:
  0.0 2.5 %shuffle_first.1 = (bf16[4,2,512,128]{3,2,1,0:T(8,128)(2,1)}, bf16[4,2,512,128]{3,2,1,0:T(8,128)(2,1)}) custom-call(bf16[512,1536]{1,0:T(8,128)(2,1)} %refs_0_.3, bf16[512,1536]{1,0:T(8,128)(2,1)} %refs_1_.3), custom_call_target="tpu_custom_call" | custom-call | bytes 4194304 | tf_op jit(solution)/shard_map/shuffle_first/pallas_call | solution.py:156
  2.5 2.4 %collective-permute-start = (bf16[4,2,512,128]{3,2,1,0:T(8,128)(2,1)}, bf16[4,2,512,128]{3,2,1,0:T(8,128)(2,1)}, u32[]{:S(2)}, u32[]{:S(2)}) collective-permute-start(bf16[4,2,512,128]{3,2,1,0:T(8,128)(2,1)} %get-tuple-element.40), channel_id=1, source_target_pairs={{4,8},{8,4},{5,9},{9,5},{6,10},{10,6},{7,11},{11,7},{20,24},{24,20... | collective-permute-start | bytes 3145736 | tf_op jit(solution)/shard_map/cross_raw_2/ppermute | solution.py:321
  4.9 18.0 %all_to_all.40 = bf16[4,2,512,128]{3,2,1,0:T(8,128)(2,1)S(1)} all-to-all(bf16[4,2,512,128]{3,2,1,0:T(8,128)(2,1)} %get-tuple-element.32), channel_id=1, replica_groups=mesh['groups'=2,'z'=4,'y'=2,'head'=2] {'y','head'}, dimensions={0} | all-to-all | bytes 2097152 | tf_op jit(solution)/shard_map/all_to_all | solution.py:317
  24.1 3.5 %collective-permute-start.1 = (bf16[4,2,512,128]{3,2,1,0:T(8,128)(2,1)S(1)}, bf16[4,2,512,128]{3,2,1,0:T(8,128)(2,1)S(1)}, u32[]{:S(2)}, u32[]{:S(2)}) collective-permute-start(bf16[4,2,512,128]{3,2,1,0:T(8,128)(2,1)S(1)} %all_to_all.40), channel_id=1, source_target_pairs={{4,8},{8,4},{5,9},{9,5},{6,10},{10,6},{7,11},{11,7},{20,24},{24,20... | collective-permute-start | bytes 3145736 | tf_op jit(solution)/shard_map/cross_0/ppermute | solution.py:321
  27.6 2.7 %shuffle_rest.1 = (bf16[4,2,512,128]{3,2,1,0:T(8,128)(2,1)}, bf16[4,1,512,128]{3,2,1,0:T(8,128)(2,1)}, bf16[4,2,512,128]{3,2,1,0:T(8,128)(2,1)}) custom-call(bf16[512,1536]{1,0:T(8,128)(2,1)} %refs_0_.2, bf16[512,1536]{1,0:T(8,128)(2,1)} %refs_0_.3, bf16[512,1536]{1,0:T(8,128)(2,1)} %refs_1_.3), custom_call_target="tpu_custom_call" | custom-call | bytes 5242880 | tf_op jit(solution)/shard_map/shuffle_rest/pallas_call | solution.py:156
  30.6 18.8 %all_to_all.41 = bf16[4,2,512,128]{3,2,1,0:T(8,128)(2,1)} all-to-all(bf16[4,2,512,128]{3,2,1,0:T(8,128)(2,1)} %get-tuple-element.34), channel_id=1, replica_groups=mesh['groups'=2,'z'=4,'y'=2,'head'=2] {'y','head'}, dimensions={0} | all-to-all | bytes 2097152 | tf_op jit(solution)/shard_map/all_to_all | solution.py:317
  49.7 2.3 %collective-permute-done.1 = bf16[4,2,512,128]{3,2,1,0:T(8,128)(2,1)S(1)} collective-permute-done((bf16[4,2,512,128]{3,2,1,0:T(8,128)(2,1)S(1)}, bf16[4,2,512,128]{3,2,1,0:T(8,128)(2,1)S(1)}, u32[]{:S(2)}, u32[]{:S(2)}) %collective-permute-start.1) | collective-permute-done | bytes 1048608 | tf_op jit(solution)/shard_map/cross_0/ppermute | solution.py:321
  52.0 4.3 %all-to-all-start.2 = ((bf16[4,1,512,128]{3,2,1,0:T(8,128)(2,1)}), bf16[4,1,512,128]{3,2,1,0:T(8,128)(2,1)}, u32[]{:S(2)}, u32[]{:S(2)}) async-start(bf16[4,1,512,128]{3,2,1,0:T(8,128)(2,1)} %get-tuple-element.35), calls=%async_computation.2 | async-start | bytes 1048576 | tf_op jit(solution)/shard_map/all_to_all | solution.py:317
  56.3 2.5 %collective-permute-start.4 = (bf16[4,2,512,128]{3,2,1,0:T(8,128)(2,1)S(1)}, bf16[4,2,512,128]{3,2,1,0:T(8,128)(2,1)}, u32[]{:S(2)}, u32[]{:S(2)}) collective-permute-start(bf16[4,2,512,128]{3,2,1,0:T(8,128)(2,1)S(1)} %collective-permute-done.2), channel_id=1, source_target_pairs={{4,8},{8,4},{5,9},{9,5},{6,10},{10,6},{7,11},{11,7},{20,24},{24,20... | collective-permute-start | bytes 3145736 | tf_op jit(solution)/shard_map/relay_0/ppermute | solution.py:321
  60.0 5.1 %all-to-all-done.2 = bf16[4,1,512,128]{3,2,1,0:T(8,128)(2,1)} async-done(((bf16[4,1,512,128]{3,2,1,0:T(8,128)(2,1)}), bf16[4,1,512,128]{3,2,1,0:T(8,128)(2,1)}, u32[]{:S(2)}, u32[]{:S(2)}) %all-to-all-start.2) | async-done | bytes 524320 | tf_op jit(solution)/shard_map/all_to_all | solution.py:317
  65.2 3.5 %all-to-all-start.3 = ((bf16[4,2,512,128]{3,2,1,0:T(8,128)(2,1)}), bf16[4,2,512,128]{3,2,1,0:T(8,128)(2,1)S(1)}, u32[]{:S(2)}, u32[]{:S(2)}) async-start(bf16[4,2,512,128]{3,2,1,0:T(8,128)(2,1)} %get-tuple-element.40), calls=%async_computation.3 | async-start | bytes 2097152 | tf_op jit(solution)/shard_map/all_to_all | solution.py:317
  69.6 2.4 %collective-permute-start.8 = (bf16[4,2,512,128]{3,2,1,0:T(8,128)(2,1)}, bf16[4,2,512,128]{3,2,1,0:T(8,128)(2,1)}, u32[]{:S(2)}, u32[]{:S(2)}) collective-permute-start(bf16[4,2,512,128]{3,2,1,0:T(8,128)(2,1)} %all_to_all.41), channel_id=1, source_target_pairs={{4,8},{8,4},{5,9},{9,5},{6,10},{10,6},{7,11},{11,7},{20,24},{24,20... | collective-permute-start | bytes 3145736 | tf_op jit(solution)/shard_map/cross_1/ppermute | solution.py:321
  73.4 10.9 %collective-permute-done.4 = bf16[4,2,512,128]{3,2,1,0:T(8,128)(2,1)} collective-permute-done((bf16[4,2,512,128]{3,2,1,0:T(8,128)(2,1)S(1)}, bf16[4,2,512,128]{3,2,1,0:T(8,128)(2,1)}, u32[]{:S(2)}, u32[]{:S(2)}) %collective-permute-start.4) | collective-permute-done | bytes 1048608 | tf_op jit(solution)/shard_map/relay_0/ppermute | solution.py:321
  84.2 2.7 %collective-permute-done.7 = bf16[4,2,512,128]{3,2,1,0:T(8,128)(2,1)} collective-permute-done((bf16[4,2,512,128]{3,2,1,0:T(8,128)(2,1)}, bf16[4,2,512,128]{3,2,1,0:T(8,128)(2,1)}, u32[]{:S(2)}, u32[]{:S(2)}) %collective-permute-start.7) | collective-permute-done | bytes 1048608 | tf_op jit(solution)/shard_map/in_1/ppermute | solution.py:321
  86.9 3.4 %collective-permute-start.9 = (bf16[4,2,512,128]{3,2,1,0:T(8,128)(2,1)}, bf16[4,2,512,128]{3,2,1,0:T(8,128)(2,1)}, u32[]{:S(2)}, u32[]{:S(2)}) collective-permute-start(bf16[4,2,512,128]{3,2,1,0:T(8,128)(2,1)} %collective-permute-done.7), channel_id=1, source_target_pairs={{4,8},{8,4},{5,9},{9,5},{6,10},{10,6},{7,11},{11,7},{20,24},{24,20... | collective-permute-start | bytes 3145736 | tf_op jit(solution)/shard_map/relay_1/ppermute | solution.py:321
  90.3 3.5 %all-to-all-start.4 = ((bf16[4,2,512,128]{3,2,1,0:T(8,128)(2,1)}), bf16[4,2,512,128]{3,2,1,0:T(8,128)(2,1)S(1)}, u32[]{:S(2)}, u32[]{:S(2)}) async-start(bf16[4,2,512,128]{3,2,1,0:T(8,128)(2,1)} %get-tuple-element.41), calls=%async_computation.4 | async-start | bytes 2097152 | tf_op jit(solution)/shard_map/all_to_all | solution.py:317
  95.2 10.7 %attend_00.1 = bf16[32,64,128]{2,1,0:T(8,128)(2,1)} custom-call(s32[1]{0:T(128)} %bitcast.count, s32[32,24]{1,0:T(8,128)} %get-tuple-element.55.lists, bf16[4,1,8,64,128]{4,3,2,1,0:T(8,128)(2,1)} %bitcast.5.query, bf16[4,2,8,64,128]{4,3,2,1,0:T(8,128)(2,1)} %bitcast.49, bf16[4,2,8,64,128]{4,3,2,1,0:T(8,128)(2,1)} %bitcast.55, ...), custom_call_target="tpu_custom_call" | custom-call | flops 8999999488 | bytes 1 | tf_op jit(solution)/shard_map/attend_00/pallas_call | solution.py:286
  105.9 2.4 %all-to-all-done.4 = bf16[4,2,512,128]{3,2,1,0:T(8,128)(2,1)S(1)} async-done(((bf16[4,2,512,128]{3,2,1,0:T(8,128)(2,1)}), bf16[4,2,512,128]{3,2,1,0:T(8,128)(2,1)S(1)}, u32[]{:S(2)}, u32[]{:S(2)}) %all-to-all-start.4) | async-done | bytes 1048608 | tf_op jit(solution)/shard_map/all_to_all | solution.py:317
  109.3 3.5 %all-to-all-start.5 = ((bf16[4,2,512,128]{3,2,1,0:T(8,128)(2,1)}), bf16[4,2,512,128]{3,2,1,0:T(8,128)(2,1)S(1)}, u32[]{:S(2)}, u32[]{:S(2)}) async-start(bf16[4,2,512,128]{3,2,1,0:T(8,128)(2,1)} %collective-permute-done), calls=%async_computation.5 | async-start | bytes 2097152 | tf_op jit(solution)/shard_map/all_to_all | solution.py:317
  114.1 10.7 %attend_01.1 = bf16[32,64,128]{2,1,0:T(8,128)(2,1)} custom-call(s32[1]{0:T(128)} %bitcast.count, s32[32,24]{1,0:T(8,128)} %get-tuple-element.56.lists, bf16[4,1,8,64,128]{4,3,2,1,0:T(8,128)(2,1)} %bitcast.10.query, bf16[4,2,8,64,128]{4,3,2,1,0:T(8,128)(2,1)} %bitcast.51, bf16[4,2,8,64,128]{4,3,2,1,0:T(8,128)(2,1)} %bitcast.57, ...), custom_call_target="tpu_custom_call" | custom-call | flops 8999999488 | bytes 1 | tf_op jit(solution)/shard_map/attend_01/pallas_call | solution.py:286
  124.8 2.1 %collective-permute-start.5 = (bf16[32,64,128]{2,1,0:T(8,128)(2,1)}, bf16[32,64,128]{2,1,0:T(8,128)(2,1)}, u32[]{:S(2)}, u32[]{:S(2)}) collective-permute-start(bf16[32,64,128]{2,1,0:T(8,128)(2,1)} %attend_01.1), channel_id=1, source_target_pairs={{4,0},{8,12},{5,1},{9,13},{6,2},{10,14},{7,3},{11,15},{20,16},{24,... | collective-permute-start | bytes 1572872 | tf_op jit(solution)/shard_map/out_0/ppermute | solution.py:321
  126.9 2.4 %collective-permute-start.12 = (bf16[4,2,512,128]{3,2,1,0:T(8,128)(2,1)S(1)}, bf16[4,2,512,128]{3,2,1,0:T(8,128)(2,1)S(1)}, u32[]{:S(2)}, u32[]{:S(2)}) collective-permute-start(bf16[4,2,512,128]{3,2,1,0:T(8,128)(2,1)S(1)} %collective-permute-done.11), channel_id=1, source_target_pairs={{4,8},{8,4},{5,9},{9,5},{6,10},{10,6},{7,11},{11,7},{20,24},{24,20... | collective-permute-start | bytes 3145736 | tf_op jit(solution)/shard_map/relay_2/ppermute | solution.py:321
  129.4 10.7 %attend_10.1 = bf16[32,64,128]{2,1,0:T(8,128)(2,1)} custom-call(s32[1]{0:T(128)} %bitcast.count, s32[32,24]{1,0:T(8,128)} %get-tuple-element.55.lists, bf16[4,2,8,64,128]{4,3,2,1,0:T(8,128)(2,1)} %bitcast.44, bf16[4,2,8,64,128]{4,3,2,1,0:T(8,128)(2,1)} %bitcast.13.refs_0_.refs_4_, bf16[4,2,8,64,128]{4,3,2,1,0:T(8,128)(2,1)} %bitcast.14.refs_1_.refs_5_, ...), custom_call_target="tpu_custom_call" | custom-call | flops 8999999488 | bytes 1 | tf_op jit(solution)/shard_map/attend_10/pallas_call | solution.py:286
  140.2 3.7 %collective-permute-done.6 = bf16[4,2,512,128]{3,2,1,0:T(8,128)(2,1)} collective-permute-done((bf16[4,2,512,128]{3,2,1,0:T(8,128)(2,1)}, bf16[4,2,512,128]{3,2,1,0:T(8,128)(2,1)}, u32[]{:S(2)}, u32[]{:S(2)}) %collective-permute-start.6) | collective-permute-done | bytes 1048608 | tf_op jit(solution)/shard_map/in_q/ppermute | solution.py:321
  143.9 10.8 %attend_11.1 = bf16[32,64,128]{2,1,0:T(8,128)(2,1)} custom-call(s32[1]{0:T(128)} %bitcast.count, s32[32,24]{1,0:T(8,128)} %get-tuple-element.56.lists, bf16[4,2,8,64,128]{4,3,2,1,0:T(8,128)(2,1)} %bitcast.17.query, bf16[4,2,8,64,128]{4,3,2,1,0:T(8,128)(2,1)} %bitcast.13.refs_0_.refs_4_, bf16[4,2,8,64,128]{4,3,2,1,0:T(8,128)(2,1)} %bitcast.14.refs_1_.refs_5_, ...), custom_call_target="tpu_custom_call" | custom-call | flops 24000000000 | bytes 1 | tf_op jit(solution)/shard_map/attend_11/pallas_call | solution.py:286
  157.1 10.8 %attend_21.1 = bf16[32,64,128]{2,1,0:T(8,128)(2,1)} custom-call(s32[1]{0:T(128)} %bitcast.count, s32[32,24]{1,0:T(8,128)} %get-tuple-element.56.lists, bf16[4,2,8,64,128]{4,3,2,1,0:T(8,128)(2,1)} %bitcast.18.query, bf16[4,2,8,64,128]{4,3,2,1,0:T(8,128)(2,1)} %bitcast.28, bf16[4,2,8,64,128]{4,3,2,1,0:T(8,128)(2,1)} %bitcast.36, ...), custom_call_target="tpu_custom_call" | custom-call | flops 1 | bytes 1 | tf_op jit(solution)/shard_map/attend_21/pallas_call | solution.py:286
  168.0 1.3 collective-permute-start.13
  170.5 3.5 %all-to-all-start.6 = ((bf16[4,2,512,128]{3,2,1,0:T(8,128)(2,1)}), bf16[4,2,512,128]{3,2,1,0:T(8,128)(2,1)S(1)}, u32[]{:S(2)}, u32[]{:S(2)}) async-start(bf16[4,2,512,128]{3,2,1,0:T(8,128)(2,1)} %pad_maximum_fusion), calls=%async_computation.6 | async-start | bytes 2097152 | tf_op jit(solution)/shard_map/all_to_all | solution.py:317
  174.0 10.7 %attend_20.1 = bf16[32,64,128]{2,1,0:T(8,128)(2,1)} custom-call(s32[1]{0:T(128)} %bitcast.count, s32[32,24]{1,0:T(8,128)} %get-tuple-element.55.lists, bf16[4,2,8,64,128]{4,3,2,1,0:T(8,128)(2,1)} %bitcast.45, bf16[4,2,8,64,128]{4,3,2,1,0:T(8,128)(2,1)} %bitcast.30, bf16[4,2,8,64,128]{4,3,2,1,0:T(8,128)(2,1)} %bitcast.38, ...), custom_call_target="tpu_custom_call" | custom-call | flops 1 | bytes 1 | tf_op jit(solution)/shard_map/attend_20/pallas_call | solution.py:286
  185.8 2.6 %all-to-all-done.6.refs_0_ = bf16[4,2,512,128]{3,2,1,0:T(8,128)(2,1)S(1)} async-done(((bf16[4,2,512,128]{3,2,1,0:T(8,128)(2,1)}), bf16[4,2,512,128]{3,2,1,0:T(8,128)(2,1)S(1)}, u32[]{:S(2)}, u32[]{:S(2)}) %all-to-all-start.6) | async-done | bytes 1048608 | tf_op jit(solution)/shard_map/all_to_all | solution.py:317
  188.4 11.9 %all_to_all.42.refs_1_ = bf16[4,1,512,128]{3,2,1,0:T(8,128)(2,1)} all-to-all(bf16[4,1,512,128]{3,2,1,0:T(8,128)(2,1)S(1)} %bitcast.46), channel_id=1, replica_groups=mesh['groups'=2,'z'=4,'y'=2,'head'=2] {'y','head'}, dimensions={0} | all-to-all | bytes 1048576 | tf_op jit(solution)/shard_map/all_to_all | solution.py:317
  200.3 2.3 %gather_out.1 = bf16[512,1536]{1,0:T(8,128)(2,1)} custom-call(bf16[4,2,512,128]{3,2,1,0:T(8,128)(2,1)} %copy-done.5, bf16[4,1,512,128]{3,2,1,0:T(8,128)(2,1)} %all_to_all.42.refs_1_), custom_call_target="tpu_custom_call" | custom-call | flops 1 | bytes 1 | tf_op jit(solution)/shard_map/gather_out/pallas_call | solution.py:200
  (51 shorter events, 13.5 us)
Async XLA Ops:
  2.5 28.1 %collective-permute-start = (bf16[4,2,512,128]{3,2,1,0:T(8,128)(2,1)}, bf16[4,2,512,128]{3,2,1,0:T(8,128)(2,1)}, u32[]{:S(2)}, u32[]{:S(2)}) collective-permute-start(bf16[4,2,512,128]{3,2,1,0:T(8,128)(2,1)} %get-tuple-element.40), channel_id=1, source_target_pairs={{4,8},{8,4},{5,9},{9,5},{6,10},{10,6},{7,11},{11,7},{20,24},{24,20... | collective-permute-start | bytes 3145736 | tf_op jit(solution)/shard_map/cross_raw_2/ppermute | solution.py:321
  22.8 7.5 %copy-start.6 = (bf16[4,2,512,128]{3,2,1,0:T(8,128)(2,1)}, bf16[4,2,512,128]{3,2,1,0:T(8,128)(2,1)S(1)}, u32[]{:S(2)}) copy-start(bf16[4,2,512,128]{3,2,1,0:T(8,128)(2,1)S(1)} %all_to_all.40) | copy-start | bytes 3145732
  22.8 26.8 %collective-permute-start.2 = (bf16[4,2,512,128]{3,2,1,0:T(8,128)(2,1)S(1)}, bf16[4,2,512,128]{3,2,1,0:T(8,128)(2,1)S(1)}, u32[]{:S(2)}, u32[]{:S(2)}) collective-permute-start(bf16[4,2,512,128]{3,2,1,0:T(8,128)(2,1)S(1)} %all_to_all.40), channel_id=1, source_target_pairs={{0,4},{12,8},{1,5},{13,9},{2,6},{14,10},{3,7},{15,11},{16,20},{28,... | collective-permute-start | bytes 3145736 | tf_op jit(solution)/shard_map/in_0/ppermute | solution.py:321
  24.1 27.9 %collective-permute-start.1 = (bf16[4,2,512,128]{3,2,1,0:T(8,128)(2,1)S(1)}, bf16[4,2,512,128]{3,2,1,0:T(8,128)(2,1)S(1)}, u32[]{:S(2)}, u32[]{:S(2)}) collective-permute-start(bf16[4,2,512,128]{3,2,1,0:T(8,128)(2,1)S(1)} %all_to_all.40), channel_id=1, source_target_pairs={{4,8},{8,4},{5,9},{9,5},{6,10},{10,6},{7,11},{11,7},{20,24},{24,20... | collective-permute-start | bytes 3145736 | tf_op jit(solution)/shard_map/cross_0/ppermute | solution.py:321
  49.7 15.5 %copy-start.10 = (bf16[4,2,512,128]{3,2,1,0:T(8,128)(2,1)}, bf16[4,2,512,128]{3,2,1,0:T(8,128)(2,1)S(1)}, u32[]{:S(2)}) copy-start(bf16[4,2,512,128]{3,2,1,0:T(8,128)(2,1)S(1)} %collective-permute-done.2) | copy-start | bytes 3145732
  52.0 13.2 %copy-start.11 = (bf16[4,2,512,128]{3,2,1,0:T(8,128)(2,1)}, bf16[4,2,512,128]{3,2,1,0:T(8,128)(2,1)S(1)}, u32[]{:S(2)}) copy-start(bf16[4,2,512,128]{3,2,1,0:T(8,128)(2,1)S(1)} %collective-permute-done.1) | copy-start | bytes 3145732
  52.0 16.7 %copy-start.9 = (s32[128,24]{0,1:T(8,128)S(1)}, s32[128,24]{0,1:T(8,128)}, u32[]{:S(2)}) copy-start(s32[128,24]{0,1:T(8,128)} %param.7) | copy-start | bytes 36868
  52.0 13.2 %all-to-all-start.2 = ((bf16[4,1,512,128]{3,2,1,0:T(8,128)(2,1)}), bf16[4,1,512,128]{3,2,1,0:T(8,128)(2,1)}, u32[]{:S(2)}, u32[]{:S(2)}) async-start(bf16[4,1,512,128]{3,2,1,0:T(8,128)(2,1)} %get-tuple-element.35), calls=%async_computation.2 | async-start | bytes 1048576 | tf_op jit(solution)/shard_map/all_to_all | solution.py:317
  56.3 28.0 %collective-permute-start.4 = (bf16[4,2,512,128]{3,2,1,0:T(8,128)(2,1)S(1)}, bf16[4,2,512,128]{3,2,1,0:T(8,128)(2,1)}, u32[]{:S(2)}, u32[]{:S(2)}) collective-permute-start(bf16[4,2,512,128]{3,2,1,0:T(8,128)(2,1)S(1)} %collective-permute-done.2), channel_id=1, source_target_pairs={{4,8},{8,4},{5,9},{9,5},{6,10},{10,6},{7,11},{11,7},{20,24},{24,20... | collective-permute-start | bytes 3145736 | tf_op jit(solution)/shard_map/relay_0/ppermute | solution.py:321
  58.7 28.2 %collective-permute-start.7 = (bf16[4,2,512,128]{3,2,1,0:T(8,128)(2,1)}, bf16[4,2,512,128]{3,2,1,0:T(8,128)(2,1)}, u32[]{:S(2)}, u32[]{:S(2)}) collective-permute-start(bf16[4,2,512,128]{3,2,1,0:T(8,128)(2,1)} %all_to_all.41), channel_id=1, source_target_pairs={{0,4},{12,8},{1,5},{13,9},{2,6},{14,10},{3,7},{15,11},{16,20},{28,... | collective-permute-start | bytes 3145736 | tf_op jit(solution)/shard_map/in_1/ppermute | solution.py:321
  65.2 25.2 %all-to-all-start.3 = ((bf16[4,2,512,128]{3,2,1,0:T(8,128)(2,1)}), bf16[4,2,512,128]{3,2,1,0:T(8,128)(2,1)S(1)}, u32[]{:S(2)}, u32[]{:S(2)}) async-start(bf16[4,2,512,128]{3,2,1,0:T(8,128)(2,1)} %get-tuple-element.40), calls=%async_computation.3 | async-start | bytes 2097152 | tf_op jit(solution)/shard_map/all_to_all | solution.py:317
  69.6 57.3 %collective-permute-start.8 = (bf16[4,2,512,128]{3,2,1,0:T(8,128)(2,1)}, bf16[4,2,512,128]{3,2,1,0:T(8,128)(2,1)}, u32[]{:S(2)}, u32[]{:S(2)}) collective-permute-start(bf16[4,2,512,128]{3,2,1,0:T(8,128)(2,1)} %all_to_all.41), channel_id=1, source_target_pairs={{4,8},{8,4},{5,9},{9,5},{6,10},{10,6},{7,11},{11,7},{20,24},{24,20... | collective-permute-start | bytes 3145736 | tf_op jit(solution)/shard_map/cross_1/ppermute | solution.py:321
  72.1 33.9 %collective-permute-start.3 = (bf16[4,1,512,128]{3,2,1,0:T(8,128)(2,1)}, bf16[4,1,512,128]{3,2,1,0:T(8,128)(2,1)}, u32[]{:S(2)}, u32[]{:S(2)}) collective-permute-start(bf16[4,1,512,128]{3,2,1,0:T(8,128)(2,1)} %all-to-all-done.2), channel_id=1, source_target_pairs={{0,4},{12,8},{1,5},{13,9},{2,6},{14,10},{3,7},{15,11},{16,20},{28,... | collective-permute-start | bytes 1572872 | tf_op jit(solution)/shard_map/in_q0/ppermute | solution.py:321
  86.9 42.5 %collective-permute-start.9 = (bf16[4,2,512,128]{3,2,1,0:T(8,128)(2,1)}, bf16[4,2,512,128]{3,2,1,0:T(8,128)(2,1)}, u32[]{:S(2)}, u32[]{:S(2)}) collective-permute-start(bf16[4,2,512,128]{3,2,1,0:T(8,128)(2,1)} %collective-permute-done.7), channel_id=1, source_target_pairs={{4,8},{8,4},{5,9},{9,5},{6,10},{10,6},{7,11},{11,7},{20,24},{24,20... | collective-permute-start | bytes 3145736 | tf_op jit(solution)/shard_map/relay_1/ppermute | solution.py:321
  90.3 15.6 %copy-start = (bf16[4,2,512,128]{3,2,1,0:T(8,128)(2,1)}, bf16[4,2,512,128]{3,2,1,0:T(8,128)(2,1)S(1)}, u32[]{:S(2)}) copy-start(bf16[4,2,512,128]{3,2,1,0:T(8,128)(2,1)S(1)} %all-to-all-done.3) | copy-start | bytes 3145732
  90.3 18.0 %all-to-all-start.4 = ((bf16[4,2,512,128]{3,2,1,0:T(8,128)(2,1)}), bf16[4,2,512,128]{3,2,1,0:T(8,128)(2,1)S(1)}, u32[]{:S(2)}, u32[]{:S(2)}) async-start(bf16[4,2,512,128]{3,2,1,0:T(8,128)(2,1)} %get-tuple-element.41), calls=%async_computation.4 | async-start | bytes 2097152 | tf_op jit(solution)/shard_map/all_to_all | solution.py:317
  93.9 33.1 %collective-permute-start.11 = (bf16[4,2,512,128]{3,2,1,0:T(8,128)(2,1)S(1)}, bf16[4,2,512,128]{3,2,1,0:T(8,128)(2,1)S(1)}, u32[]{:S(2)}, u32[]{:S(2)}) collective-permute-start(bf16[4,2,512,128]{3,2,1,0:T(8,128)(2,1)S(1)} %all-to-all-done.3), channel_id=1, source_target_pairs={{0,4},{12,8},{1,5},{13,9},{2,6},{14,10},{3,7},{15,11},{16,20},{28,... | collective-permute-start | bytes 3145736 | tf_op jit(solution)/shard_map/in_2/ppermute | solution.py:321
  108.3 1.0 copy-start.4
  109.3 20.1 %all-to-all-start.5 = ((bf16[4,2,512,128]{3,2,1,0:T(8,128)(2,1)}), bf16[4,2,512,128]{3,2,1,0:T(8,128)(2,1)S(1)}, u32[]{:S(2)}, u32[]{:S(2)}) async-start(bf16[4,2,512,128]{3,2,1,0:T(8,128)(2,1)} %collective-permute-done), calls=%async_computation.5 | async-start | bytes 2097152 | tf_op jit(solution)/shard_map/all_to_all | solution.py:317
  112.8 31.1 %collective-permute-start.6 = (bf16[4,2,512,128]{3,2,1,0:T(8,128)(2,1)}, bf16[4,2,512,128]{3,2,1,0:T(8,128)(2,1)}, u32[]{:S(2)}, u32[]{:S(2)}) collective-permute-start(bf16[4,2,512,128]{3,2,1,0:T(8,128)(2,1)} %copy-done.4), channel_id=1, source_target_pairs={{0,4},{12,8},{1,5},{13,9},{2,6},{14,10},{3,7},{15,11},{16,20},{28,... | collective-permute-start | bytes 3145736 | tf_op jit(solution)/shard_map/in_q/ppermute | solution.py:321
  124.8 31.2 %collective-permute-start.5 = (bf16[32,64,128]{2,1,0:T(8,128)(2,1)}, bf16[32,64,128]{2,1,0:T(8,128)(2,1)}, u32[]{:S(2)}, u32[]{:S(2)}) collective-permute-start(bf16[32,64,128]{2,1,0:T(8,128)(2,1)} %attend_01.1), channel_id=1, source_target_pairs={{4,0},{8,12},{5,1},{9,13},{6,2},{10,14},{7,3},{11,15},{20,16},{24,... | collective-permute-start | bytes 1572872 | tf_op jit(solution)/shard_map/out_0/ppermute | solution.py:321
  126.9 13.2 %copy-start.2 = (bf16[4,2,512,128]{3,2,1,0:T(8,128)(2,1)}, bf16[4,2,512,128]{3,2,1,0:T(8,128)(2,1)S(1)}, u32[]{:S(2)}) copy-start(bf16[4,2,512,128]{3,2,1,0:T(8,128)(2,1)S(1)} %collective-permute-done.11) | copy-start | bytes 3145732
  126.9 29.2 %collective-permute-start.12 = (bf16[4,2,512,128]{3,2,1,0:T(8,128)(2,1)S(1)}, bf16[4,2,512,128]{3,2,1,0:T(8,128)(2,1)S(1)}, u32[]{:S(2)}, u32[]{:S(2)}) collective-permute-start(bf16[4,2,512,128]{3,2,1,0:T(8,128)(2,1)S(1)} %collective-permute-done.11), channel_id=1, source_target_pairs={{4,8},{8,4},{5,9},{9,5},{6,10},{10,6},{7,11},{11,7},{20,24},{24,20... | collective-permute-start | bytes 3145736 | tf_op jit(solution)/shard_map/relay_2/ppermute | solution.py:321
  129.4 10.8 %copy-start.1 = (bf16[4,2,512,128]{3,2,1,0:T(8,128)(2,1)}, bf16[4,2,512,128]{3,2,1,0:T(8,128)(2,1)S(1)}, u32[]{:S(2)}) copy-start(bf16[4,2,512,128]{3,2,1,0:T(8,128)(2,1)S(1)} %all-to-all-done.5) | copy-start | bytes 3145732
  143.9 12.2 %copy-start.7 = (bf16[32,64,128]{2,1,0:T(8,128)(2,1)S(1)}, bf16[32,64,128]{2,1,0:T(8,128)(2,1)}, u32[]{:S(2)}) copy-start(bf16[32,64,128]{2,1,0:T(8,128)(2,1)} %attend_00.1) | copy-start | bytes 1572868
  154.7 14.6 %collective-permute-start.10 = (bf16[32,64,128]{2,1,0:T(8,128)(2,1)}, bf16[32,64,128]{2,1,0:T(8,128)(2,1)S(1)}, u32[]{:S(2)}, u32[]{:S(2)}) collective-permute-start(bf16[32,64,128]{2,1,0:T(8,128)(2,1)} %attend_11.1), channel_id=1, source_target_pairs={{4,0},{8,12},{5,1},{9,13},{6,2},{10,14},{7,3},{11,15},{20,16},{24,... | collective-permute-start | bytes 1572872 | tf_op jit(solution)/shard_map/out_1/ppermute | solution.py:321
  156.1 1.0 copy-start.3
  157.1 12.2 %copy-start.8 = (bf16[32,64,128]{2,1,0:T(8,128)(2,1)S(1)}, bf16[32,64,128]{2,1,0:T(8,128)(2,1)}, u32[]{:S(2)}) copy-start(bf16[32,64,128]{2,1,0:T(8,128)(2,1)} %attend_10.1) | copy-start | bytes 1572868
  168.0 16.8 %collective-permute-start.13 = (bf16[32,64,128]{2,1,0:T(8,128)(2,1)}, bf16[32,64,128]{2,1,0:T(8,128)(2,1)S(1)}, u32[]{:S(2)}, u32[]{:S(2)}) collective-permute-start(bf16[32,64,128]{2,1,0:T(8,128)(2,1)} %attend_21.1), channel_id=1, source_target_pairs={{4,0},{8,12},{5,1},{9,13},{6,2},{10,14},{7,3},{11,15},{20,16},{24,... | collective-permute-start | bytes 1572872 | tf_op jit(solution)/shard_map/out_2/ppermute | solution.py:321
  170.5 18.0 %all-to-all-start.6 = ((bf16[4,2,512,128]{3,2,1,0:T(8,128)(2,1)}), bf16[4,2,512,128]{3,2,1,0:T(8,128)(2,1)S(1)}, u32[]{:S(2)}, u32[]{:S(2)}) async-start(bf16[4,2,512,128]{3,2,1,0:T(8,128)(2,1)} %pad_maximum_fusion), calls=%async_computation.6 | async-start | bytes 2097152 | tf_op jit(solution)/shard_map/all_to_all | solution.py:317
  188.4 11.9 %copy-start.5 = (bf16[4,2,512,128]{3,2,1,0:T(8,128)(2,1)}, bf16[4,2,512,128]{3,2,1,0:T(8,128)(2,1)S(1)}, u32[]{:S(2)}) copy-start(bf16[4,2,512,128]{3,2,1,0:T(8,128)(2,1)S(1)} %all-to-all-done.6.refs_0_) | copy-start | bytes 3145732

commit v2 on v1

--- a/solution.py
+++ b/solution.py
@@ -111,6 +111,7 @@
 SIDE = 2
 AXES = ("groups", "z", "y", "head")
 RANKS = ("y", "head")
+SWAP = [(0, 1), (1, 0), (2, 3), (3, 2)]
 INWARD = [(0, 1), (3, 2)]
 OUTWARD = [(1, 0), (2, 3)]
 CROSS = [(1, 2), (2, 1)]
@@ -213,9 +214,8 @@
     )(*parts, *given)
 
 
-def attend_kernel(count, lists, query, *refs, chunk, ats):
-    picks = refs[: 2 * PLANES]
-    out, query_buf, key_buf, value_buf, score_buf, sems = refs[2 * PLANES :]
+def attend_kernel(flags, lists, query, *refs, chunk, ats, forwarded):
+    out, query_buf, key_buf, value_buf, score_buf, sems = refs[-6:]
     lanes, _, shard_tiles = query.shape[:3]
     tiles = lanes * shard_tiles
     top_count = lists.shape[1]
@@ -224,17 +224,37 @@
     def beside(left, right):
         return jnp.concatenate([left, right], axis=1)
 
-    @pl.when(count[0] > 0)
+    @pl.when(flags[0] != 0)
     def _():
         shaped = (lanes, shard_tiles, TILE, HD)
         pltpu.make_async_copy(query.at[:, chunk], query_buf.reshape(shaped), sems.at[0]).start()
-        for kind, buf in enumerate((key_buf, value_buf)):
-            for slot in range(PLANES):
-                pltpu.make_async_copy(
-                    picks[kind * PLANES + slot].at[:, ats[kind]],
-                    buf.reshape((PLANES, *shaped)).at[slot],
-                    sems.at[1 + kind],
-                ).start()
+        def load(which, kind, slot):
+            buf = (key_buf, value_buf)[kind]
+            pltpu.make_async_copy(
+                refs[which].at[:, ats[which]],
+                buf.reshape((PLANES, *shaped)).at[slot],
+                sems.at[1 + kind],
+            ).start()
+
+        for kind in range(2):
+            for slot in range(PLANES if forwarded == 0 else PLANES - forwarded):
+                load(kind * PLANES + slot, kind, slot)
+
+        if forwarded > 0:
+
+            @pl.when(flags[1] == 0)
+            def _():
+                for kind in range(2):
+                    for slot in range(PLANES - forwarded, PLANES):
+                        load(kind * PLANES + slot, kind, slot)
+
+            @pl.when(flags[1] != 0)
+            def _():
+                for kind in range(2):
+                    for at in range(forwarded):
+                        which = 2 * PLANES + kind * forwarded + at
+                        load(which, kind, PLANES - forwarded + at)
+
         pltpu.make_async_copy(query_buf, query_buf, sems.at[0]).wait()
         pltpu.make_async_copy(key_buf, key_buf, sems.at[1]).wait()
 
@@ -279,15 +299,17 @@
         lax.fori_loop(0, tiles // 2 // unroll, step, 0)
 
 
-def attend(count, lists, query, keys, values, ats, chunk, cost, name):
+def attend(flags, lists, query, keys, values, ats, chunk, cost, name):
     tiles, top_count = lists.shape
     lanes = query.shape[0]
     shaped = (lanes, -1, tiles // lanes, TILE, HD)
+    forwarded = len(keys) - PLANES
+    picks = [*keys[:PLANES], *values[:PLANES], *keys[PLANES:], *values[PLANES:]]
     return pl.pallas_call(
-        functools.partial(attend_kernel, chunk=chunk, ats=ats),
+        functools.partial(attend_kernel, chunk=chunk, ats=ats, forwarded=forwarded),
         out_shape=jax.ShapeDtypeStruct((tiles, TILE, HD), jnp.bfloat16),
         in_specs=[pl.BlockSpec(memory_space=pltpu.SMEM)] * 2
-        + [pl.BlockSpec(memory_space=pl.ANY)] * (1 + 2 * PLANES),
+        + [pl.BlockSpec(memory_space=pl.ANY)] * (1 + len(picks)),
         out_specs=pl.BlockSpec(memory_space=pltpu.VMEM),
         scratch_shapes=[
             pltpu.VMEM((tiles, TILE, HD), jnp.bfloat16),
@@ -299,7 +321,7 @@
         compiler_params=pltpu.CompilerParams(vmem_limit_bytes=VMEM_LIMIT),
         cost_estimate=pl.CostEstimate(flops=cost, bytes_accessed=1, transcendentals=0),
         name=name,
-    )(count, lists, query.reshape(shaped), *[a.reshape(shaped) for a in (*keys, *values)])
+    )(flags, lists, query.reshape(shaped), *[a.reshape(shaped) for a in picks])
 
 
 def after(array, *others):
@@ -332,38 +354,41 @@
     near = jnp.where(far, PLANES - 1 - z, z)
     slot = jnp.where(plane < 2, plane ^ near, plane)
     lists = slot * plane_tiles + rows % plane_tiles
-    count = jnp.where(at_end, 0, 1).astype(jnp.int32).reshape(1)
+    ends = at_end.astype(jnp.int32)
+    inner, everyone = jnp.stack([1 - ends, 0 * ends]), jnp.stack([0 * ends + 1, ends])
 
     first, rest_2 = shuffle(
         [keys, values], lanes, [[(0, 0), (1, 0)], [(0, 2), (1, 2)]], "shuffle_first"
     )
     raw_2 = send(rest_2, CROSS, "cross_raw_2")
     own_0 = swap(first)
-    rest_1, rest_q0, rest_q = shuffle(
+    rest_1, rest_q = shuffle(
         [queries, keys, values],
         lanes,
-        [[(1, 1), (2, 1)], [(0, 0)], [(0, 1), (0, 2)]],
+        [[(1, 1), (2, 1)], [(0, c) for c in range(chunks)]],
         "shuffle_rest",
     )
-    in_0 = send(own_0, INWARD, "in_0")
+    in_0 = send(own_0, SWAP, "in_0")
     cross_0 = send(own_0, CROSS, "cross_0")
     own_1 = swap(after(rest_1, own_0, raw_2))
     relay_0 = send(after(in_0, cross_0), CROSS, "relay_0")
     in_1 = send(after(own_1, in_0), INWARD, "in_1")
     cross_1 = send(after(own_1, cross_0), CROSS, "cross_1")
-    asked_0 = swap(after(rest_q0, own_1, cross_0, in_0))
-    in_q0 = send(after(asked_0, in_0), INWARD, "in_q0")
-    own_2 = swap(after(rest_2, asked_0))
-    relay_1 = send(after(in_1, relay_0), CROSS, "relay_1")
+    out_cross = send(cross_0, OUTWARD, "out_cross_0")
+    own_2 = swap(after(rest_2, own_1, cross_0, in_0))
+    out_relay = send(relay_0, OUTWARD, "out_relay_0")
+    relay_1 = send(after(in_1, relay_0, out_cross), CROSS, "relay_1")
     in_2 = send(after(own_2, in_1), INWARD, "in_2")
     asked = swap(after(rest_q, own_2))
-    in_q = send(after(asked, in_q0), INWARD, "in_q")
+    in_q = send(after(asked[:, 1:], in_1), INWARD, "in_q")
     cross_2 = swap(after(raw_2, asked))
     relay_2 = send(after(in_2, cross_1), CROSS, "relay_2")
 
     def one(at, chunk, query, pairs, place, cost=COST):
         name = f"attend_{chunk}{at}"
-        return attend(count, lists[at], query, pairs, pairs, (0, 1), place, cost, name)
+        ats = ((0,) * PLANES + (1,) * PLANES) + (0,) * (len(pairs) - PLANES) + (1,) * (len(pairs) - PLANES)
+        flags = inner if len(pairs) == PLANES else everyone
+        return attend(flags, lists[at], query, pairs, pairs, ats, place, cost, name)
 
     def home(beside, chunk):
         return send(beside, OUTWARD, f"out_{chunk}")
@@ -374,21 +399,19 @@
             mixed.append(jnp.where(at_end, home, own).reshape(lanes, -1, HD))
         return mixed[0][:, None] if len(mixed) == 1 else jnp.stack(mixed, axis=1)
 
-    pairs = [own_0, in_0, cross_0, relay_0]
-    mine_0 = one(0, 0, asked_0, pairs, 0)
-    theirs_0 = one(1, 0, after(in_q0, mine_0), pairs, 0)
-    home_0 = home(theirs_0, 0)
+    pairs = [own_0, in_0, cross_0, relay_0, out_cross, out_relay]
+    mine_0 = one(0, 0, asked, pairs, 0)
+    early_0 = swap(mine_0.reshape(lanes, 1, -1, HD))
     pairs = [own_1, in_1, cross_1, relay_1]
-    mine_1 = one(0, 1, after(asked, theirs_0, cross_2), pairs, 0)
+    mine_1 = one(0, 1, after(asked, mine_0, cross_2), pairs, 1)
     theirs_1 = one(1, 1, after(in_q, mine_1), pairs, 0, LONG)
     home_1 = home(theirs_1, 1)
     pairs = [own_2, in_2, cross_2, relay_2]
-    theirs_2 = one(1, 2, after(in_q, theirs_1), pairs, 1, 1)
-    mixed = finish([(mine_0, home_0), (mine_1, after(home_1, theirs_2))])
-    early = swap(mixed)
-    mine_2 = one(0, 2, after(asked, theirs_2), pairs, 1, 1)
+    theirs_2 = one(1, 2, after(in_q, theirs_1, early_0), pairs, 1, 1)
+    early = swap(after(finish([(mine_1, after(home_1, theirs_2))]), early_0))
+    mine_2 = one(0, 2, after(asked, theirs_2), pairs, 2, 1)
     late = swap(after(finish([(mine_2, home(theirs_2, 2))]), early))
-    return gather_out([early, late], 0, chunks * lanes, None, "gather_out")
+    return gather_out([early_0, early, late], 0, chunks * lanes, None, "gather_out")
 
 
 def solution(mesh):

time: 206 us -> 197 us (0.956)
  Pallas kernels: 72.1 us -> 61.3 us
  waiting for transfers between devices: 30.3 us -> 24.2 us
  starting transfers between devices: 46.1 us -> 52.1 us
    ppermute x14, waiting for transfers between devices: 20.1 us -> 9.04 us  [send(): return lax.ppermute(array, 'z', pairs)]
    pallas_call x6 -> x5, Pallas kernels: 64.6 us -> 53.8 us  [attend(): pl.pallas_call(functools.partial(attend_kernel, chunk=chunk, ats=ats, for...]
    ppermute x14, starting transfers between devices: 27.7 us -> 32.9 us  [send(): return lax.ppermute(array, 'z', pairs)]
    all_to_all x5, waiting for transfers between devices: 10.1 us -> 15.2 us  [swap(): return lax.all_to_all(array, RANKS, split_axis=0, concat_axis=0, tiled=True)]
    slice x0 -> x1, local copies, waits for them, and re-layouts: none -> 2.28 us  [relay_plan(): in_q = send(after(asked[:, 1:], in_1), INWARD, 'in_q')]
  transfers between devices with their start and end apart: 19 -> 19, of which waited for: 9 -> 7; matrix products, arithmetic and copies ran while one was open for 2% -> 3% of each run, Pallas kernels for 33% -> 29%
where the time goes in v2:
time: 197 us; the launch traced here: 194 us
  Pallas kernels  61.3 us (31%)
  starting transfers between devices  52.1 us (26%)
  blocking collectives  48.8 us (25%)
  waiting for transfers between devices  24.2 us (12%)
  local copies, waits for them, and re-layouts  4.11 us (2%)
  other arithmetic  3.31 us (2%)
    pallas_call x5, Pallas kernels, attend(): pl.pallas_call(functools.partial(attend_kernel, chunk=chunk, ats=ats, for...  53.8 us
    all_to_all x3, blocking collectives, swap(): return lax.all_to_all(array, RANKS, split_axis=0, concat_axis=0, tiled=True)  48.8 us
    ppermute x14, starting transfers between devices, send(): return lax.ppermute(array, 'z', pairs)  32.9 us
    all_to_all x5, starting transfers between devices, swap(): return lax.all_to_all(array, RANKS, split_axis=0, concat_axis=0, tiled=True)  19.1 us
    all_to_all x5, waiting for transfers between devices, swap(): return lax.all_to_all(array, RANKS, split_axis=0, concat_axis=0, tiled=True)  15.2 us
    ppermute x14, waiting for transfers between devices, send(): return lax.ppermute(array, 'z', pairs)  9.04 us
    pallas_call x2, Pallas kernels, shuffle(): pl.pallas_call(kernel, out_shape=[jax.ShapeDtypeStruct((lanes, len(p), ro...  5.24 us
  transfers between devices with their start and end apart: 19, of which 7 were waited for; matrix products, arithmetic and copies ran while one was open for 3% of the time, Pallas kernels for 29%

profile of v2, /device:TPU:18, one launch (start us, length us, event | category | flops | bytes accessed | tf_op | source)
XLA Modules:
  0.0 194.1 jit_solution(11521394727534988748)
XLA Ops:
  0.0 2.5 %shuffle_first.1 = (bf16[4,2,512,128]{3,2,1,0:T(8,128)(2,1)}, bf16[4,2,512,128]{3,2,1,0:T(8,128)(2,1)}) custom-call(bf16[512,1536]{1,0:T(8,128)(2,1)} %refs_0_.3, bf16[512,1536]{1,0:T(8,128)(2,1)} %refs_1_.3), custom_call_target="tpu_custom_call" | custom-call | bytes 4194304 | tf_op jit(solution)/shard_map/shuffle_first/pallas_call | solution.py:157
  2.5 2.4 %collective-permute-start = (bf16[4,2,512,128]{3,2,1,0:T(8,128)(2,1)}, bf16[4,2,512,128]{3,2,1,0:T(8,128)(2,1)S(1)}, u32[]{:S(2)}, u32[]{:S(2)}) collective-permute-start(bf16[4,2,512,128]{3,2,1,0:T(8,128)(2,1)} %get-tuple-element.32), channel_id=1, source_target_pairs={{4,8},{8,4},{5,9},{9,5},{6,10},{10,6},{7,11},{11,7},{20,24},{24,20... | collective-permute-start | bytes 3145736 | tf_op jit(solution)/shard_map/cross_raw_2/ppermute | solution.py:343
  4.9 18.0 %all_to_all.40 = bf16[4,2,512,128]{3,2,1,0:T(8,128)(2,1)S(1)} all-to-all(bf16[4,2,512,128]{3,2,1,0:T(8,128)(2,1)} %get-tuple-element.30), channel_id=1, replica_groups=mesh['groups'=2,'z'=4,'y'=2,'head'=2] {'y','head'}, dimensions={0} | all-to-all | bytes 2097152 | tf_op jit(solution)/shard_map/all_to_all | solution.py:339
  22.8 3.5 %collective-permute-start.1 = (bf16[4,2,512,128]{3,2,1,0:T(8,128)(2,1)S(1)}, bf16[4,2,512,128]{3,2,1,0:T(8,128)(2,1)}, u32[]{:S(2)}, u32[]{:S(2)}) collective-permute-start(bf16[4,2,512,128]{3,2,1,0:T(8,128)(2,1)S(1)} %all_to_all.40), channel_id=1, source_target_pairs={{4,8},{8,4},{5,9},{9,5},{6,10},{10,6},{7,11},{11,7},{20,24},{24,20... | collective-permute-start | bytes 3145736 | tf_op jit(solution)/shard_map/cross_0/ppermute | solution.py:343
  26.3 2.7 %shuffle_rest.1 = (bf16[4,2,512,128]{3,2,1,0:T(8,128)(2,1)}, bf16[4,3,512,128]{3,2,1,0:T(8,128)(2,1)}) custom-call(bf16[512,1536]{1,0:T(8,128)(2,1)} %refs_0_.2, bf16[512,1536]{1,0:T(8,128)(2,1)} %refs_0_.3, bf16[512,1536]{1,0:T(8,128)(2,1)} %refs_1_.3), custom_call_target="tpu_custom_call" | custom-call | bytes 5242880 | tf_op jit(solution)/shard_map/shuffle_rest/pallas_call | solution.py:157
  29.1 1.6 collective-permute-done
  30.7 18.8 %all_to_all.41 = bf16[4,2,512,128]{3,2,1,0:T(8,128)(2,1)} all-to-all(bf16[4,2,512,128]{3,2,1,0:T(8,128)(2,1)} %get-tuple-element.31), channel_id=1, replica_groups=mesh['groups'=2,'z'=4,'y'=2,'head'=2] {'y','head'}, dimensions={0} | all-to-all | bytes 2097152 | tf_op jit(solution)/shard_map/all_to_all | solution.py:339
  50.7 1.4 collective-permute-done.1
  52.1 2.3 %collective-permute-start.3 = (bf16[4,2,512,128]{3,2,1,0:T(8,128)(2,1)S(1)}, bf16[4,2,512,128]{3,2,1,0:T(8,128)(2,1)}, u32[]{:S(2)}, u32[]{:S(2)}) collective-permute-start(bf16[4,2,512,128]{3,2,1,0:T(8,128)(2,1)S(1)} %collective-permute-done.2), channel_id=1, source_target_pairs={{4,8},{8,4},{5,9},{9,5},{6,10},{10,6},{7,11},{11,7},{20,24},{24,20... | collective-permute-start | bytes 3145736 | tf_op jit(solution)/shard_map/relay_0/ppermute | solution.py:343
  54.5 3.5 %all-to-all-start.2 = ((bf16[4,2,512,128]{3,2,1,0:T(8,128)(2,1)}), bf16[4,2,512,128]{3,2,1,0:T(8,128)(2,1)S(1)}, u32[]{:S(2)}, u32[]{:S(2)}) async-start(bf16[4,2,512,128]{3,2,1,0:T(8,128)(2,1)} %get-tuple-element.32), calls=%async_computation.2 | async-start | bytes 2097152 | tf_op jit(solution)/shard_map/all_to_all | solution.py:339
  58.0 4.5 %collective-permute-start.4 = (bf16[4,2,512,128]{3,2,1,0:T(8,128)(2,1)}, bf16[4,2,512,128]{3,2,1,0:T(8,128)(2,1)}, u32[]{:S(2)}, u32[]{:S(2)}) collective-permute-start(bf16[4,2,512,128]{3,2,1,0:T(8,128)(2,1)} %collective-permute-done.1), channel_id=1, source_target_pairs={{4,0},{8,12},{5,1},{9,13},{6,2},{10,14},{7,3},{11,15},{20,16},{24,... | collective-permute-start | bytes 3145736 | tf_op jit(solution)/shard_map/out_cross_0/ppermute | solution.py:343
  62.5 10.0 %all-to-all-done.2 = bf16[4,2,512,128]{3,2,1,0:T(8,128)(2,1)S(1)} async-done(((bf16[4,2,512,128]{3,2,1,0:T(8,128)(2,1)}), bf16[4,2,512,128]{3,2,1,0:T(8,128)(2,1)S(1)}, u32[]{:S(2)}, u32[]{:S(2)}) %all-to-all-start.2) | async-done | bytes 1048608 | tf_op jit(solution)/shard_map/all_to_all | solution.py:339
  72.4 4.5 %all-to-all-start.3 = ((bf16[4,3,512,128]{3,2,1,0:T(8,128)(2,1)}), bf16[4,3,512,128]{3,2,1,0:T(8,128)(2,1)}, u32[]{:S(2)}, u32[]{:S(2)}) async-start(bf16[4,3,512,128]{3,2,1,0:T(8,128)(2,1)} %get-tuple-element.33), calls=%async_computation.3 | async-start | bytes 3145728 | tf_op jit(solution)/shard_map/all_to_all | solution.py:339
  76.9 3.5 %collective-permute-start.8 = (bf16[4,2,512,128]{3,2,1,0:T(8,128)(2,1)}, bf16[4,2,512,128]{3,2,1,0:T(8,128)(2,1)}, u32[]{:S(2)}, u32[]{:S(2)}) collective-permute-start(bf16[4,2,512,128]{3,2,1,0:T(8,128)(2,1)} %all_to_all.41), channel_id=1, source_target_pairs={{4,8},{8,4},{5,9},{9,5},{6,10},{10,6},{7,11},{11,7},{20,24},{24,20... | collective-permute-start | bytes 3145736 | tf_op jit(solution)/shard_map/cross_1/ppermute | solution.py:343
  81.7 5.6 %collective-permute-start.5 = (bf16[4,2,512,128]{3,2,1,0:T(8,128)(2,1)}, bf16[4,2,512,128]{3,2,1,0:T(8,128)(2,1)}, u32[]{:S(2)}, u32[]{:S(2)}) collective-permute-start(bf16[4,2,512,128]{3,2,1,0:T(8,128)(2,1)} %collective-permute-done.3), channel_id=1, source_target_pairs={{4,0},{8,12},{5,1},{9,13},{6,2},{10,14},{7,3},{11,15},{20,16},{24,... | collective-permute-start | bytes 3145736 | tf_op jit(solution)/shard_map/out_relay_0/ppermute | solution.py:343
  88.9 2.4 %collective-permute-start.9 = (bf16[4,2,512,128]{3,2,1,0:T(8,128)(2,1)}, bf16[4,2,512,128]{3,2,1,0:T(8,128)(2,1)}, u32[]{:S(2)}, u32[]{:S(2)}) collective-permute-start(bf16[4,2,512,128]{3,2,1,0:T(8,128)(2,1)} %collective-permute-done.6), channel_id=1, source_target_pairs={{4,8},{8,4},{5,9},{9,5},{6,10},{10,6},{7,11},{11,7},{20,24},{24,20... | collective-permute-start | bytes 3145736 | tf_op jit(solution)/shard_map/relay_1/ppermute | solution.py:343
  91.9 5.2 %all-to-all-done.3 = bf16[4,3,512,128]{3,2,1,0:T(8,128)(2,1)} async-done(((bf16[4,3,512,128]{3,2,1,0:T(8,128)(2,1)}), bf16[4,3,512,128]{3,2,1,0:T(8,128)(2,1)}, u32[]{:S(2)}, u32[]{:S(2)}) %all-to-all-start.3) | async-done | bytes 1572896 | tf_op jit(solution)/shard_map/all_to_all | solution.py:339
  97.1 3.5 %all-to-all-start.5 = ((bf16[4,2,512,128]{3,2,1,0:T(8,128)(2,1)}), bf16[4,2,512,128]{3,2,1,0:T(8,128)(2,1)S(1)}, u32[]{:S(2)}, u32[]{:S(2)}) async-start(bf16[4,2,512,128]{3,2,1,0:T(8,128)(2,1)} %copy-done.5), calls=%async_computation.5 | async-start | bytes 2097152 | tf_op jit(solution)/shard_map/all_to_all | solution.py:339
  100.6 2.3 %slice.17 = bf16[4,2,512,128]{3,2,1,0:T(8,128)(2,1)} slice(bf16[4,3,512,128]{3,2,1,0:T(8,128)(2,1)} %all-to-all-done.3), slice={[0:4], [1:3], [0:512], [0:128]} | slice | bytes 2097152 | tf_op jit(solution)/shard_map/slice | solution.py:383
  105.1 2.5 %collective-permute-done.11 = bf16[4,2,512,128]{3,2,1,0:T(8,128)(2,1)S(1)} collective-permute-done((bf16[4,2,512,128]{3,2,1,0:T(8,128)(2,1)S(1)}, bf16[4,2,512,128]{3,2,1,0:T(8,128)(2,1)S(1)}, u32[]{:S(2)}, u32[]{:S(2)}) %collective-permute-start.11) | collective-permute-done | bytes 1048608 | tf_op jit(solution)/shard_map/in_2/ppermute | solution.py:343
  107.6 2.3 %collective-permute-start.12 = (bf16[4,2,512,128]{3,2,1,0:T(8,128)(2,1)S(1)}, bf16[4,2,512,128]{3,2,1,0:T(8,128)(2,1)S(1)}, u32[]{:S(2)}, u32[]{:S(2)}) collective-permute-start(bf16[4,2,512,128]{3,2,1,0:T(8,128)(2,1)S(1)} %collective-permute-done.11), channel_id=1, source_target_pairs={{4,8},{8,4},{5,9},{9,5},{6,10},{10,6},{7,11},{11,7},{20,24},{24,20... | collective-permute-start | bytes 3145736 | tf_op jit(solution)/shard_map/relay_2/ppermute | solution.py:343
  109.9 10.8 %attend_00.1 = bf16[32,64,128]{2,1,0:T(8,128)(2,1)} custom-call(s32[2]{0:T(128)} %pad_add_fusion.1.flags, s32[32,24]{1,0:T(8,128)} %get-tuple-element.50.lists, bf16[4,3,8,64,128]{4,3,2,1,0:T(8,128)(2,1)} %bitcast.4.query, bf16[4,2,8,64,128]{4,3,2,1,0:T(8,128)(2,1)} %bitcast.47, bf16[4,2,8,64,128]{4,3,2,1,0:T(8,128)(2,1)} %bitcast.52, ...), custom_call_target="tpu_custom_call" | custom-call | flops 8999999488 | bytes 1 | tf_op jit(solution)/shard_map/attend_00/pallas_call | solution.py:308
  120.8 4.1 %all-to-all-start.4 = ((bf16[4,1,512,128]{3,2,1,0:T(8,128)(2,1)}), bf16[4,1,512,128]{3,2,1,0:T(8,128)(2,1)}, u32[]{:S(2)}, u32[]{:S(2)}) async-start(bf16[4,1,512,128]{3,2,1,0:T(8,128)(2,1)} %bitcast.49), calls=%async_computation.4 | async-start | bytes 1048576 | tf_op jit(solution)/shard_map/all_to_all | solution.py:339
  124.9 2.6 %collective-permute-done.9 = bf16[4,2,512,128]{3,2,1,0:T(8,128)(2,1)} collective-permute-done((bf16[4,2,512,128]{3,2,1,0:T(8,128)(2,1)}, bf16[4,2,512,128]{3,2,1,0:T(8,128)(2,1)}, u32[]{:S(2)}, u32[]{:S(2)}) %collective-permute-start.9) | collective-permute-done | bytes 1048608 | tf_op jit(solution)/shard_map/relay_1/ppermute | solution.py:343
  127.6 10.7 %attend_10.1 = bf16[32,64,128]{2,1,0:T(8,128)(2,1)} custom-call(s32[2]{0:T(128)} %pad_add_fusion.2.flags, s32[32,24]{1,0:T(8,128)} %get-tuple-element.50.lists, bf16[4,3,8,64,128]{4,3,2,1,0:T(8,128)(2,1)} %bitcast.14.query, bf16[4,2,8,64,128]{4,3,2,1,0:T(8,128)(2,1)} %bitcast.15.refs_0_.refs_4_, bf16[4,2,8,64,128]{4,3,2,1,0:T(8,128)(2,1)} %bitcast.16.refs_1_.refs_5_, ...), custom_call_target="tpu_custom_call" | custom-call | flops 8999999488 | bytes 1 | tf_op jit(solution)/shard_map/attend_10/pallas_call | solution.py:308
  138.3 10.7 %attend_11.1 = bf16[32,64,128]{2,1,0:T(8,128)(2,1)} custom-call(s32[2]{0:T(128)} %pad_add_fusion.2.flags, s32[32,24]{1,0:T(8,128)} %get-tuple-element.49.lists, bf16[4,2,8,64,128]{4,3,2,1,0:T(8,128)(2,1)} %bitcast.19.query, bf16[4,2,8,64,128]{4,3,2,1,0:T(8,128)(2,1)} %bitcast.15.refs_0_.refs_4_, bf16[4,2,8,64,128]{4,3,2,1,0:T(8,128)(2,1)} %bitcast.16.refs_1_.refs_5_, ...), custom_call_target="tpu_custom_call" | custom-call | flops 24000000000 | bytes 1 | tf_op jit(solution)/shard_map/attend_11/pallas_call | solution.py:308
  149.0 1.3 collective-permute-start.10
  151.4 10.8 %attend_21.1 = bf16[32,64,128]{2,1,0:T(8,128)(2,1)} custom-call(s32[2]{0:T(128)} %pad_add_fusion.2.flags, s32[32,24]{1,0:T(8,128)} %get-tuple-element.49.lists, bf16[4,2,8,64,128]{4,3,2,1,0:T(8,128)(2,1)} %bitcast.20.query, bf16[4,2,8,64,128]{4,3,2,1,0:T(8,128)(2,1)} %bitcast.30, bf16[4,2,8,64,128]{4,3,2,1,0:T(8,128)(2,1)} %bitcast.38, ...), custom_call_target="tpu_custom_call" | custom-call | flops 1 | bytes 1 | tf_op jit(solution)/shard_map/attend_21/pallas_call | solution.py:308
  164.4 3.5 %all-to-all-start.6 = ((bf16[4,1,512,128]{3,2,1,0:T(8,128)(2,1)}), bf16[4,1,512,128]{3,2,1,0:T(8,128)(2,1)S(1)}, u32[]{:S(2)}, u32[]{:S(2)}) async-start(bf16[4,1,512,128]{3,2,1,0:T(8,128)(2,1)} %bitcast.25), calls=%async_computation.6 | async-start | bytes 1048576 | tf_op jit(solution)/shard_map/all_to_all | solution.py:339
  167.9 10.7 %attend_20.1 = bf16[32,64,128]{2,1,0:T(8,128)(2,1)} custom-call(s32[2]{0:T(128)} %pad_add_fusion.2.flags, s32[32,24]{1,0:T(8,128)} %get-tuple-element.50.lists, bf16[4,3,8,64,128]{4,3,2,1,0:T(8,128)(2,1)} %bitcast.26.query, bf16[4,2,8,64,128]{4,3,2,1,0:T(8,128)(2,1)} %bitcast.32, bf16[4,2,8,64,128]{4,3,2,1,0:T(8,128)(2,1)} %bitcast.40, ...), custom_call_target="tpu_custom_call" | custom-call | flops 1 | bytes 1 | tf_op jit(solution)/shard_map/attend_20/pallas_call | solution.py:308
  179.8 12.0 %all_to_all.42.refs_2_ = bf16[4,1,512,128]{3,2,1,0:T(8,128)(2,1)} all-to-all(bf16[4,1,512,128]{3,2,1,0:T(8,128)(2,1)S(1)} %bitcast.46), channel_id=1, replica_groups=mesh['groups'=2,'z'=4,'y'=2,'head'=2] {'y','head'}, dimensions={0} | all-to-all | bytes 1048576 | tf_op jit(solution)/shard_map/all_to_all | solution.py:339
  191.8 2.3 %gather_out.1 = bf16[512,1536]{1,0:T(8,128)(2,1)} custom-call(bf16[4,1,512,128]{3,2,1,0:T(8,128)(2,1)} %all-to-all-done.4.refs_0_, bf16[4,1,512,128]{3,2,1,0:T(8,128)(2,1)} %copy-done.4, bf16[4,1,512,128]{3,2,1,0:T(8,128)(2,1)} %all_to_all.42.refs_2_), custom_call_target="tpu_custom_call" | custom-call | flops 1 | bytes 1 | tf_op jit(solution)/shard_map/gather_out/pallas_call | solution.py:201
  (47 shorter events, 11.3 us)
Async XLA Ops:
  2.5 28.1 %collective-permute-start = (bf16[4,2,512,128]{3,2,1,0:T(8,128)(2,1)}, bf16[4,2,512,128]{3,2,1,0:T(8,128)(2,1)S(1)}, u32[]{:S(2)}, u32[]{:S(2)}) collective-permute-start(bf16[4,2,512,128]{3,2,1,0:T(8,128)(2,1)} %get-tuple-element.32), channel_id=1, source_target_pairs={{4,8},{8,4},{5,9},{9,5},{6,10},{10,6},{7,11},{11,7},{20,24},{24,20... | collective-permute-start | bytes 3145736 | tf_op jit(solution)/shard_map/cross_raw_2/ppermute | solution.py:343
  22.8 6.2 %copy-start.6 = (bf16[4,2,512,128]{3,2,1,0:T(8,128)(2,1)}, bf16[4,2,512,128]{3,2,1,0:T(8,128)(2,1)S(1)}, u32[]{:S(2)}) copy-start(bf16[4,2,512,128]{3,2,1,0:T(8,128)(2,1)S(1)} %all_to_all.40) | copy-start | bytes 3145732
  22.8 26.6 %collective-permute-start.2 = (bf16[4,2,512,128]{3,2,1,0:T(8,128)(2,1)S(1)}, bf16[4,2,512,128]{3,2,1,0:T(8,128)(2,1)S(1)}, u32[]{:S(2)}, u32[]{:S(2)}) collective-permute-start(bf16[4,2,512,128]{3,2,1,0:T(8,128)(2,1)S(1)} %all_to_all.40), channel_id=1, source_target_pairs={{0,4},{4,0},{8,12},{12,8},{1,5},{5,1},{9,13},{13,9},{2,6},{6,2},{1... | collective-permute-start | bytes 3145736 | tf_op jit(solution)/shard_map/in_0/ppermute | solution.py:343
  22.8 29.2 %collective-permute-start.1 = (bf16[4,2,512,128]{3,2,1,0:T(8,128)(2,1)S(1)}, bf16[4,2,512,128]{3,2,1,0:T(8,128)(2,1)}, u32[]{:S(2)}, u32[]{:S(2)}) collective-permute-start(bf16[4,2,512,128]{3,2,1,0:T(8,128)(2,1)S(1)} %all_to_all.40), channel_id=1, source_target_pairs={{4,8},{8,4},{5,9},{9,5},{6,10},{10,6},{7,11},{11,7},{20,24},{24,20... | collective-permute-start | bytes 3145736 | tf_op jit(solution)/shard_map/cross_0/ppermute | solution.py:343
  30.7 23.8 %copy-start.5 = (bf16[4,2,512,128]{3,2,1,0:T(8,128)(2,1)}, bf16[4,2,512,128]{3,2,1,0:T(8,128)(2,1)S(1)}, u32[]{:S(2)}) copy-start(bf16[4,2,512,128]{3,2,1,0:T(8,128)(2,1)S(1)} %collective-permute-done) | copy-start | bytes 3145732
  49.4 23.0 %copy-start.9 = (bf16[4,2,512,128]{3,2,1,0:T(8,128)(2,1)}, bf16[4,2,512,128]{3,2,1,0:T(8,128)(2,1)S(1)}, u32[]{:S(2)}) copy-start(bf16[4,2,512,128]{3,2,1,0:T(8,128)(2,1)S(1)} %collective-permute-done.2) | copy-start | bytes 3145732
  49.4 31.0 %collective-permute-start.6 = (bf16[4,2,512,128]{3,2,1,0:T(8,128)(2,1)}, bf16[4,2,512,128]{3,2,1,0:T(8,128)(2,1)}, u32[]{:S(2)}, u32[]{:S(2)}) collective-permute-start(bf16[4,2,512,128]{3,2,1,0:T(8,128)(2,1)} %all_to_all.41), channel_id=1, source_target_pairs={{0,4},{12,8},{1,5},{13,9},{2,6},{14,10},{3,7},{15,11},{16,20},{28,... | collective-permute-start | bytes 3145736 | tf_op jit(solution)/shard_map/in_1/ppermute | solution.py:343
  52.1 29.6 %collective-permute-start.3 = (bf16[4,2,512,128]{3,2,1,0:T(8,128)(2,1)S(1)}, bf16[4,2,512,128]{3,2,1,0:T(8,128)(2,1)}, u32[]{:S(2)}, u32[]{:S(2)}) collective-permute-start(bf16[4,2,512,128]{3,2,1,0:T(8,128)(2,1)S(1)} %collective-permute-done.2), channel_id=1, source_target_pairs={{4,8},{8,4},{5,9},{9,5},{6,10},{10,6},{7,11},{11,7},{20,24},{24,20... | collective-permute-start | bytes 3145736 | tf_op jit(solution)/shard_map/relay_0/ppermute | solution.py:343
  54.5 18.0 %all-to-all-start.2 = ((bf16[4,2,512,128]{3,2,1,0:T(8,128)(2,1)}), bf16[4,2,512,128]{3,2,1,0:T(8,128)(2,1)S(1)}, u32[]{:S(2)}, u32[]{:S(2)}) async-start(bf16[4,2,512,128]{3,2,1,0:T(8,128)(2,1)} %get-tuple-element.32), calls=%async_computation.2 | async-start | bytes 2097152 | tf_op jit(solution)/shard_map/all_to_all | solution.py:339
  58.0 30.9 %collective-permute-start.4 = (bf16[4,2,512,128]{3,2,1,0:T(8,128)(2,1)}, bf16[4,2,512,128]{3,2,1,0:T(8,128)(2,1)}, u32[]{:S(2)}, u32[]{:S(2)}) collective-permute-start(bf16[4,2,512,128]{3,2,1,0:T(8,128)(2,1)} %collective-permute-done.1), channel_id=1, source_target_pairs={{4,0},{8,12},{5,1},{9,13},{6,2},{10,14},{7,3},{11,15},{20,16},{24,... | collective-permute-start | bytes 3145736 | tf_op jit(solution)/shard_map/out_cross_0/ppermute | solution.py:343
  72.4 8.0 %copy-start = (bf16[4,2,512,128]{3,2,1,0:T(8,128)(2,1)}, bf16[4,2,512,128]{3,2,1,0:T(8,128)(2,1)S(1)}, u32[]{:S(2)}) copy-start(bf16[4,2,512,128]{3,2,1,0:T(8,128)(2,1)S(1)} %all-to-all-done.2) | copy-start | bytes 3145732
  72.4 14.9 %copy-start.8 = (s32[128,24]{0,1:T(8,128)S(1)}, s32[128,24]{0,1:T(8,128)}, u32[]{:S(2)}) copy-start(s32[128,24]{0,1:T(8,128)} %param.7) | copy-start | bytes 36868
  72.4 24.6 %all-to-all-start.3 = ((bf16[4,3,512,128]{3,2,1,0:T(8,128)(2,1)}), bf16[4,3,512,128]{3,2,1,0:T(8,128)(2,1)}, u32[]{:S(2)}, u32[]{:S(2)}) async-start(bf16[4,3,512,128]{3,2,1,0:T(8,128)(2,1)} %get-tuple-element.33), calls=%async_computation.3 | async-start | bytes 3145728 | tf_op jit(solution)/shard_map/all_to_all | solution.py:339
  76.9 28.2 %collective-permute-start.8 = (bf16[4,2,512,128]{3,2,1,0:T(8,128)(2,1)}, bf16[4,2,512,128]{3,2,1,0:T(8,128)(2,1)}, u32[]{:S(2)}, u32[]{:S(2)}) collective-permute-start(bf16[4,2,512,128]{3,2,1,0:T(8,128)(2,1)} %all_to_all.41), channel_id=1, source_target_pairs={{4,8},{8,4},{5,9},{9,5},{6,10},{10,6},{7,11},{11,7},{20,24},{24,20... | collective-permute-start | bytes 3145736 | tf_op jit(solution)/shard_map/cross_1/ppermute | solution.py:343
  80.4 27.1 %collective-permute-start.11 = (bf16[4,2,512,128]{3,2,1,0:T(8,128)(2,1)S(1)}, bf16[4,2,512,128]{3,2,1,0:T(8,128)(2,1)S(1)}, u32[]{:S(2)}, u32[]{:S(2)}) collective-permute-start(bf16[4,2,512,128]{3,2,1,0:T(8,128)(2,1)S(1)} %all-to-all-done.2), channel_id=1, source_target_pairs={{0,4},{12,8},{1,5},{13,9},{2,6},{14,10},{3,7},{15,11},{16,20},{28,... | collective-permute-start | bytes 3145736 | tf_op jit(solution)/shard_map/in_2/ppermute | solution.py:343
  81.7 28.2 %collective-permute-start.5 = (bf16[4,2,512,128]{3,2,1,0:T(8,128)(2,1)}, bf16[4,2,512,128]{3,2,1,0:T(8,128)(2,1)}, u32[]{:S(2)}, u32[]{:S(2)}) collective-permute-start(bf16[4,2,512,128]{3,2,1,0:T(8,128)(2,1)} %collective-permute-done.3), channel_id=1, source_target_pairs={{4,0},{8,12},{5,1},{9,13},{6,2},{10,14},{7,3},{11,15},{20,16},{24,... | collective-permute-start | bytes 3145736 | tf_op jit(solution)/shard_map/out_relay_0/ppermute | solution.py:343
  88.9 38.7 %collective-permute-start.9 = (bf16[4,2,512,128]{3,2,1,0:T(8,128)(2,1)}, bf16[4,2,512,128]{3,2,1,0:T(8,128)(2,1)}, u32[]{:S(2)}, u32[]{:S(2)}) collective-permute-start(bf16[4,2,512,128]{3,2,1,0:T(8,128)(2,1)} %collective-permute-done.6), channel_id=1, source_target_pairs={{4,8},{8,4},{5,9},{9,5},{6,10},{10,6},{7,11},{11,7},{20,24},{24,20... | collective-permute-start | bytes 3145736 | tf_op jit(solution)/shard_map/relay_1/ppermute | solution.py:343
  97.1 23.7 %all-to-all-start.5 = ((bf16[4,2,512,128]{3,2,1,0:T(8,128)(2,1)}), bf16[4,2,512,128]{3,2,1,0:T(8,128)(2,1)S(1)}, u32[]{:S(2)}, u32[]{:S(2)}) async-start(bf16[4,2,512,128]{3,2,1,0:T(8,128)(2,1)} %copy-done.5), calls=%async_computation.5 | async-start | bytes 2097152 | tf_op jit(solution)/shard_map/all_to_all | solution.py:339
  102.9 35.4 %collective-permute-start.7 = (bf16[4,2,512,128]{3,2,1,0:T(8,128)(2,1)}, bf16[4,2,512,128]{3,2,1,0:T(8,128)(2,1)}, u32[]{:S(2)}, u32[]{:S(2)}) collective-permute-start(bf16[4,2,512,128]{3,2,1,0:T(8,128)(2,1)} %slice.17), channel_id=1, source_target_pairs={{0,4},{12,8},{1,5},{13,9},{2,6},{14,10},{3,7},{15,11},{16,20},{28,... | collective-permute-start | bytes 3145736 | tf_op jit(solution)/shard_map/in_q/ppermute | solution.py:343
  107.6 13.2 %copy-start.2 = (bf16[4,2,512,128]{3,2,1,0:T(8,128)(2,1)}, bf16[4,2,512,128]{3,2,1,0:T(8,128)(2,1)S(1)}, u32[]{:S(2)}) copy-start(bf16[4,2,512,128]{3,2,1,0:T(8,128)(2,1)S(1)} %collective-permute-done.11) | copy-start | bytes 3145732
  107.6 42.8 %collective-permute-start.12 = (bf16[4,2,512,128]{3,2,1,0:T(8,128)(2,1)S(1)}, bf16[4,2,512,128]{3,2,1,0:T(8,128)(2,1)S(1)}, u32[]{:S(2)}, u32[]{:S(2)}) collective-permute-start(bf16[4,2,512,128]{3,2,1,0:T(8,128)(2,1)S(1)} %collective-permute-done.11), channel_id=1, source_target_pairs={{4,8},{8,4},{5,9},{9,5},{6,10},{10,6},{7,11},{11,7},{20,24},{24,20... | collective-permute-start | bytes 3145736 | tf_op jit(solution)/shard_map/relay_2/ppermute | solution.py:343
  120.8 17.5 %copy-start.1 = (bf16[4,2,512,128]{3,2,1,0:T(8,128)(2,1)}, bf16[4,2,512,128]{3,2,1,0:T(8,128)(2,1)S(1)}, u32[]{:S(2)}) copy-start(bf16[4,2,512,128]{3,2,1,0:T(8,128)(2,1)S(1)} %all-to-all-done.5) | copy-start | bytes 3145732
  120.8 29.6 %all-to-all-start.4 = ((bf16[4,1,512,128]{3,2,1,0:T(8,128)(2,1)}), bf16[4,1,512,128]{3,2,1,0:T(8,128)(2,1)}, u32[]{:S(2)}, u32[]{:S(2)}) async-start(bf16[4,1,512,128]{3,2,1,0:T(8,128)(2,1)} %bitcast.49), calls=%async_computation.4 | async-start | bytes 1048576 | tf_op jit(solution)/shard_map/all_to_all | solution.py:339
  149.0 14.5 %collective-permute-start.10 = (bf16[32,64,128]{2,1,0:T(8,128)(2,1)}, bf16[32,64,128]{2,1,0:T(8,128)(2,1)S(1)}, u32[]{:S(2)}, u32[]{:S(2)}) collective-permute-start(bf16[32,64,128]{2,1,0:T(8,128)(2,1)} %attend_11.1), channel_id=1, source_target_pairs={{4,0},{8,12},{5,1},{9,13},{6,2},{10,14},{7,3},{11,15},{20,16},{24,... | collective-permute-start | bytes 1572872 | tf_op jit(solution)/shard_map/out_1/ppermute | solution.py:343
  150.4 1.0 copy-start.3
  151.3 12.2 %copy-start.7 = (bf16[32,64,128]{2,1,0:T(8,128)(2,1)S(1)}, bf16[32,64,128]{2,1,0:T(8,128)(2,1)}, u32[]{:S(2)}) copy-start(bf16[32,64,128]{2,1,0:T(8,128)(2,1)} %attend_10.1) | copy-start | bytes 1572868
  162.2 16.5 %collective-permute-start.13 = (bf16[32,64,128]{2,1,0:T(8,128)(2,1)}, bf16[32,64,128]{2,1,0:T(8,128)(2,1)S(1)}, u32[]{:S(2)}, u32[]{:S(2)}) collective-permute-start(bf16[32,64,128]{2,1,0:T(8,128)(2,1)} %attend_21.1), channel_id=1, source_target_pairs={{4,0},{8,12},{5,1},{9,13},{6,2},{10,14},{7,3},{11,15},{20,16},{24,... | collective-permute-start | bytes 1572872 | tf_op jit(solution)/shard_map/out_2/ppermute | solution.py:343
  164.4 15.3 %all-to-all-start.6 = ((bf16[4,1,512,128]{3,2,1,0:T(8,128)(2,1)}), bf16[4,1,512,128]{3,2,1,0:T(8,128)(2,1)S(1)}, u32[]{:S(2)}, u32[]{:S(2)}) async-start(bf16[4,1,512,128]{3,2,1,0:T(8,128)(2,1)} %bitcast.25), calls=%async_computation.6 | async-start | bytes 1048576 | tf_op jit(solution)/shard_map/all_to_all | solution.py:339
  179.8 12.0 %copy-start.4 = (bf16[4,1,512,128]{3,2,1,0:T(8,128)(2,1)}, bf16[4,1,512,128]{3,2,1,0:T(8,128)(2,1)S(1)}, u32[]{:S(2)}) copy-start(bf16[4,1,512,128]{3,2,1,0:T(8,128)(2,1)S(1)} %all-to-all-done.6.refs_1_) | copy-start | bytes 1572868
